TPU v7x, 128 devices: a whole 4x4x4 slice. The times are simulated.
128 devices in a mesh: pipe: 4 (over x), dp: 32 (over z, y, core).
Axes of the slice: x: 4, y: 4, z: 4, core: 2. Of those that a mesh axis runs over, the one named last changes fastest.
Arguments:
- tokens: bfloat16 [4096, 1024], P('dp'), may hold values from -6 to 6
- cotangent: bfloat16 [4096, 1024], P('dp'), may hold values from -6 to 6
- live_counts: int32 [64], P('dp'), may hold values from 32 to 64, as said below
- segments: int32 [4096], P('dp'), may hold values from 0 to 255, never falling along the last dimension, each value on 1 to 64 neighbouring positions
- attn_input: bfloat16 [4, 1024, 3072], P('pipe', None, 'dp'), may hold values from -0.1875 to 0.1875
- attn_output: bfloat16 [4, 1024, 1024], P('pipe', None, 'dp'), may hold values from -0.1875 to 0.1875
- feed_up: bfloat16 [4, 1024, 4096], P('pipe', None, 'dp'), may hold values from -0.1875 to 0.1875
- feed_down: bfloat16 [4, 4096, 1024], P('pipe', None, 'dp'), may hold values from -0.09375 to 0.09375
- norm_gains: bfloat16 [4, 3, 1024], P('pipe', None, 'dp'), may hold values from 0.5 to 1.5
- vector_bias: bfloat16 [4, 7, 1024], P('pipe', None, 'dp'), may hold values from -2 to 2
- mid_gain: bfloat16 [4, 4096], P('pipe', 'dp'), may hold values from 0.5 to 1.5
- mid_bias: bfloat16 [4, 2, 4096], P('pipe', None, 'dp'), may hold values from -2 to 2
- head_scale: bfloat16 [4, 16], P('pipe'), may hold values from 0.25 to 1.75
Outputs:
- section_outputs: bfloat16 [4, 4096, 1024], P('pipe', 'dp')
- input_grads: bfloat16 [4, 4096, 1024], P('pipe', 'dp')
- grad_attn_input: float32 [4, 1024, 3072], P('pipe', None, 'dp')
- grad_attn_output: float32 [4, 1024, 1024], P('pipe', None, 'dp')
- grad_feed_up: float32 [4, 1024, 4096], P('pipe', None, 'dp')
- grad_feed_down: float32 [4, 4096, 1024], P('pipe', None, 'dp')
- grad_norm_gains: float32 [4, 3, 1024], P('pipe', None, 'dp')
- grad_vector_bias: float32 [4, 7, 1024], P('pipe', None, 'dp')
- grad_mid_gain: float32 [4, 4096], P('pipe', 'dp')
- grad_mid_bias: float32 [4, 2, 4096], P('pipe', None, 'dp')
- grad_head_scale: float32 [4, 16], P('pipe')
Inputs may be any that keep to these rules, and one draw needn't show every extreme that they name: `live_counts`: some pack holds 64 live tokens.
All inputs are finite; a program needn't handle non-finite values.
Results may differ from a plain program's by a relative error of at most 0.035.
Values may be sent and summed in bfloat16 or wider, within the bound.
A program may use at most 960 MiB of HBM per device.

v0:
```python
import jax
import jax.numpy as jnp
from jax import lax
from jax.sharding import PartitionSpec as P

epsilon = 1e-05


def passed_along(value, axis, by):
    devices = lax.axis_size(axis)
    pairs = [(i, i + by) for i in range(devices) if 0 <= i + by < devices]
    return lax.ppermute(value, axis, pairs)


def norm_rows(values, gain_row, bias_row):
    center = values - jnp.mean(values, axis=-1, keepdims=True)
    spread = jnp.mean(center * center, axis=-1, keepdims=True)
    return center * lax.rsqrt(spread + epsilon) * gain_row + bias_row


def inner_block(values, gain_row, bias_row):
    return norm_rows(jax.nn.gelu(values), gain_row, bias_row)


def split_heads(qkv_rows, head_count):
    num_rows = qkv_rows.shape[0]
    model_width = qkv_rows.shape[1] // 3
    head_size = model_width // head_count
    query_rows = qkv_rows[:, :model_width].reshape(num_rows, head_count, head_size)
    key_rows = qkv_rows[:, model_width : 2 * model_width].reshape(num_rows, head_count, head_size)
    value_rows = qkv_rows[:, 2 * model_width :].reshape(num_rows, head_count, head_size)
    return (query_rows, key_rows, value_rows)


def layer_forward(state, allowed, params, scales):
    (
        in_weight,
        out_weight,
        up_weight,
        down_weight,
        gains_low,
        biases_low,
        inner_gain_low,
        inner_bias_low,
    ) = params
    gains = gains_low.astype(jnp.float32)
    biases = biases_low.astype(jnp.float32)
    inner_gain = inner_gain_low.astype(jnp.float32)
    inner_bias = inner_bias_low.astype(jnp.float32)
    head_scales = scales.astype(jnp.float32)
    head_count = head_scales.shape[0]
    num_rows, model_width = state.shape
    head_size = model_width // head_count
    normed = norm_rows(state, gains[0], biases[0]).astype(jnp.bfloat16)
    qkv_bias = jnp.concatenate([biases[1], jnp.zeros_like(biases[1]), biases[2]])
    qkv_rows = (jnp.dot(normed, in_weight, preferred_element_type=jnp.float32) + qkv_bias).astype(
        jnp.bfloat16
    )
    query_rows, key_rows, value_rows = split_heads(qkv_rows, head_count)
    scores = jnp.einsum(
        "qhd,khd->hqk", query_rows, key_rows, preferred_element_type=jnp.float32
    ) * head_size ** (-0.5)
    scores = jnp.where(allowed[None], scores, -1000000000.0)
    top_score = jnp.max(scores, axis=-1, keepdims=True)
    expo_scores = jnp.exp(scores - top_score)
    attn_probs = expo_scores / jnp.sum(expo_scores, axis=-1, keepdims=True)
    probs_low = attn_probs.astype(jnp.bfloat16)
    mixed_heads = jnp.einsum(
        "hqk,khd->qhd", probs_low, value_rows, preferred_element_type=jnp.float32
    )
    scaled = (
        (mixed_heads * head_scales[None, :, None])
        .reshape(num_rows, model_width)
        .astype(jnp.bfloat16)
    )
    attn_rows = jnp.dot(scaled, out_weight, preferred_element_type=jnp.float32) + biases[3]
    middle = state + norm_rows(attn_rows, gains[1], biases[4])
    normed_two = norm_rows(middle, gains[2], biases[5]).astype(jnp.bfloat16)
    hidden = jnp.dot(normed_two, up_weight, preferred_element_type=jnp.float32) + inner_bias[0]
    inner = inner_block(hidden, inner_gain, inner_bias[1]).astype(jnp.bfloat16)
    result = middle + jnp.dot(inner, down_weight, preferred_element_type=jnp.float32) + biases[6]
    saved = (
        normed,
        qkv_rows,
        attn_probs,
        probs_low,
        mixed_heads,
        scaled,
        attn_rows,
        middle,
        normed_two,
        hidden,
        inner,
    )
    return (result, saved)


def layer_backward(state, allowed, params, scales, grad_out):
    (
        in_weight,
        out_weight,
        up_weight,
        down_weight,
        gains_low,
        biases_low,
        inner_gain_low,
        inner_bias_low,
    ) = params
    gains = gains_low.astype(jnp.float32)
    biases = biases_low.astype(jnp.float32)
    inner_gain = inner_gain_low.astype(jnp.float32)
    inner_bias = inner_bias_low.astype(jnp.float32)
    head_scales = scales.astype(jnp.float32)
    head_count = head_scales.shape[0]
    num_rows, model_width = state.shape
    head_size = model_width // head_count
    unused, saved = layer_forward(state, allowed, params, scales)
    (
        normed,
        qkv_rows,
        attn_probs,
        probs_low,
        mixed_heads,
        scaled,
        attn_rows,
        middle,
        normed_two,
        hidden,
        inner,
    ) = saved
    query_rows, key_rows, value_rows = split_heads(qkv_rows, head_count)
    grad_out_f = grad_out.astype(jnp.float32)
    grad_inner = jnp.dot(grad_out, down_weight.T, preferred_element_type=jnp.float32)
    unused_inner, inner_pull = jax.vjp(inner_block, hidden, inner_gain, inner_bias[1])
    grad_hidden, grad_inner_gain, grad_inner_bias_one = inner_pull(grad_inner)
    grad_hidden_low = grad_hidden.astype(jnp.bfloat16)
    grad_normed_two = jnp.dot(grad_hidden_low, up_weight.T, preferred_element_type=jnp.float32)
    unused_two, norm_two_pull = jax.vjp(norm_rows, middle, gains[2], biases[5])
    grad_middle_part, grad_gain_two, grad_bias_five = norm_two_pull(grad_normed_two)
    grad_middle = grad_out_f + grad_middle_part
    unused_post, post_pull = jax.vjp(norm_rows, attn_rows, gains[1], biases[4])
    grad_attn, grad_gain_one, grad_bias_four = post_pull(grad_middle)
    grad_attn_low = grad_attn.astype(jnp.bfloat16)
    grad_scaled = jnp.dot(grad_attn_low, out_weight.T, preferred_element_type=jnp.float32).reshape(
        num_rows, head_count, head_size
    )
    grad_mixed = (grad_scaled * head_scales[None, :, None]).astype(jnp.bfloat16)
    grad_probs = jnp.einsum(
        "qhd,khd->hqk", grad_mixed, value_rows, preferred_element_type=jnp.float32
    )
    row_delta = jnp.sum(attn_probs * grad_probs, axis=-1, keepdims=True)
    grad_scores = (attn_probs * (grad_probs - row_delta)).astype(jnp.bfloat16)
    score_scale = head_size ** (-0.5)
    grad_query = (
        jnp.einsum("hqk,khd->qhd", grad_scores, key_rows, preferred_element_type=jnp.float32)
        * score_scale
    )
    grad_key = (
        jnp.einsum("hqk,qhd->khd", grad_scores, query_rows, preferred_element_type=jnp.float32)
        * score_scale
    )
    grad_value = jnp.einsum(
        "hqk,qhd->khd", probs_low, grad_mixed, preferred_element_type=jnp.float32
    )
    grad_qkv = jnp.concatenate(
        [
            grad_query.reshape(num_rows, model_width),
            grad_key.reshape(num_rows, model_width),
            grad_value.reshape(num_rows, model_width),
        ],
        axis=1,
    ).astype(jnp.bfloat16)
    grad_normed = jnp.dot(grad_qkv, in_weight.T, preferred_element_type=jnp.float32)
    unused_one, norm_one_pull = jax.vjp(norm_rows, state, gains[0], biases[0])
    grad_state_part, grad_gain_zero, grad_bias_zero = norm_one_pull(grad_normed)
    grad_state = grad_middle + grad_state_part
    grad_down = jnp.dot(inner.T, grad_out, preferred_element_type=jnp.float32)
    grad_bias_six = jnp.sum(grad_out_f, axis=0)
    grad_inner_bias_zero = jnp.sum(grad_hidden_low.astype(jnp.float32), axis=0)
    grad_up = jnp.dot(normed_two.T, grad_hidden_low, preferred_element_type=jnp.float32)
    grad_bias_three = jnp.sum(grad_attn_low.astype(jnp.float32), axis=0)
    grad_out_weight = jnp.dot(scaled.T, grad_attn_low, preferred_element_type=jnp.float32)
    grad_scales = jnp.sum(grad_scaled * mixed_heads, axis=(0, 2))
    grad_qkv_f = grad_qkv.astype(jnp.float32)
    grad_bias_one = jnp.sum(grad_qkv_f[:, :model_width], axis=0)
    grad_bias_two = jnp.sum(grad_qkv_f[:, 2 * model_width :], axis=0)
    grad_in_weight = jnp.dot(normed.T, grad_qkv, preferred_element_type=jnp.float32)
    grad_gains = jnp.stack([grad_gain_zero, grad_gain_one, grad_gain_two])
    grad_biases = jnp.stack(
        [
            grad_bias_zero,
            grad_bias_one,
            grad_bias_two,
            grad_bias_three,
            grad_bias_four,
            grad_bias_five,
            grad_bias_six,
        ]
    )
    grad_inner_bias = jnp.stack([grad_inner_bias_zero, grad_inner_bias_one])
    grads = (
        grad_in_weight,
        grad_out_weight,
        grad_up,
        grad_down,
        grad_gains,
        grad_biases,
        grad_inner_gain,
        grad_inner_bias,
        grad_scales,
    )
    return (grad_state, grads)


def keep_slot(buffer, value, slot_safe, active):
    current = lax.dynamic_index_in_dim(buffer, slot_safe, 0, keepdims=False)
    updated = jnp.where(active, value, current)
    return lax.dynamic_update_index_in_dim(buffer, updated, slot_safe, 0)


def body(
    tokens,
    cotangent,
    live_counts,
    segments,
    attn_input,
    attn_output,
    feed_up,
    feed_down,
    norm_gains,
    vector_bias,
    mid_gain,
    mid_bias,
    head_scale,
):
    section_count = lax.axis_size("pipe")
    section_rank = lax.axis_index("pipe")
    group_size = lax.axis_size("dp")
    micro_count = live_counts.shape[0]
    pack_rows = tokens.shape[0] // micro_count
    model_width = tokens.shape[1]
    token_packs = tokens.reshape(micro_count, pack_rows, model_width)
    cot_packs = cotangent.reshape(micro_count, pack_rows, model_width)
    seg_packs = segments.reshape(micro_count, pack_rows)
    positions = jnp.arange(pack_rows)
    causal = positions[:, None] >= positions[None, :]
    scales = head_scale[0]
    steps_total = micro_count + section_count - 1

    def pack_mask(slot_safe):
        seg_row = lax.dynamic_index_in_dim(seg_packs, slot_safe, 0, keepdims=False)
        return causal & (seg_row[:, None] == seg_row[None, :])

    gathered = (
        lax.all_gather(attn_input[0], "dp", axis=1, tiled=True),
        lax.all_gather(attn_output[0], "dp", axis=1, tiled=True),
        lax.all_gather(feed_up[0], "dp", axis=1, tiled=True),
        lax.all_gather(feed_down[0], "dp", axis=1, tiled=True),
        lax.all_gather(norm_gains[0], "dp", axis=1, tiled=True),
        lax.all_gather(vector_bias[0], "dp", axis=1, tiled=True),
        lax.all_gather(mid_gain[0], "dp", axis=0, tiled=True),
        lax.all_gather(mid_bias[0], "dp", axis=1, tiled=True),
    )
    kept_inputs = jnp.zeros((micro_count, pack_rows, model_width), jnp.bfloat16)
    section_out = jnp.zeros((micro_count, pack_rows, model_width), jnp.bfloat16)
    incoming = jnp.zeros((pack_rows, model_width), jnp.bfloat16)
    for step_id in range(steps_total):
        slot_pos = step_id - section_rank
        active = (slot_pos >= 0) & (slot_pos < micro_count)
        slot_safe = jnp.clip(slot_pos, 0, micro_count - 1)
        own_tokens = lax.dynamic_index_in_dim(token_packs, slot_safe, 0, keepdims=False)
        layer_in = jnp.where(section_rank == 0, own_tokens, incoming)
        allowed = pack_mask(slot_safe)

        def run_forward(state_in, allowed=allowed):
            result, unused = layer_forward(state_in.astype(jnp.float32), allowed, gathered, scales)
            return result.astype(jnp.bfloat16)

        def pass_through(state_in):
            return state_in

        layer_out = lax.cond(active, run_forward, pass_through, layer_in)
        kept_inputs = keep_slot(kept_inputs, layer_in, slot_safe, active)
        section_out = keep_slot(section_out, layer_out, slot_safe, active)
        incoming = passed_along(layer_out, "pipe", 1)
    back_params = (
        lax.all_gather(attn_input[0], "dp", axis=1, tiled=True),
        lax.all_gather(attn_output[0], "dp", axis=1, tiled=True),
        lax.all_gather(feed_up[0], "dp", axis=1, tiled=True),
        lax.all_gather(feed_down[0], "dp", axis=1, tiled=True),
        lax.all_gather(norm_gains[0], "dp", axis=1, tiled=True),
        lax.all_gather(vector_bias[0], "dp", axis=1, tiled=True),
        lax.all_gather(mid_gain[0], "dp", axis=0, tiled=True),
        lax.all_gather(mid_bias[0], "dp", axis=1, tiled=True),
    )
    zero_full = tuple((jnp.zeros(p.shape, jnp.float32) for p in back_params)) + (
        jnp.zeros(scales.shape, jnp.float32),
    )
    totals = zero_full
    input_grads = jnp.zeros((micro_count, pack_rows, model_width), jnp.bfloat16)
    grad_incoming = jnp.zeros((pack_rows, model_width), jnp.bfloat16)
    for step_id in range(steps_total):
        slot_pos = step_id - (section_count - 1 - section_rank)
        active = (slot_pos >= 0) & (slot_pos < micro_count)
        slot_safe = jnp.clip(slot_pos, 0, micro_count - 1)
        kept_rows = lax.dynamic_index_in_dim(kept_inputs, slot_safe, 0, keepdims=False)
        cot_rows = lax.dynamic_index_in_dim(cot_packs, slot_safe, 0, keepdims=False)
        live_now = lax.dynamic_index_in_dim(live_counts, slot_safe, 0, keepdims=False)
        seeded = jnp.where((positions < live_now)[:, None], cot_rows, jnp.zeros_like(cot_rows))
        grad_in = jnp.where(section_rank == section_count - 1, seeded, grad_incoming)
        allowed = pack_mask(slot_safe)

        def run_backward(operands, allowed=allowed):
            grad_state, grads = layer_backward(
                operands[0].astype(jnp.float32), allowed, back_params, scales, operands[1]
            )
            return (grad_state.astype(jnp.bfloat16), grads)

        def skip_backward(operands):
            return (jnp.zeros_like(operands[0]), zero_full)

        grad_state, layer_grads = lax.cond(
            active, run_backward, skip_backward, (kept_rows, grad_in)
        )
        totals = jax.tree.map(jnp.add, totals, layer_grads)
        input_grads = keep_slot(input_grads, grad_state, slot_safe, active)
        grad_incoming = passed_along(grad_state, "pipe", -1)
    tiled_scales = jnp.tile(totals[8], group_size)
    totals = (
        lax.psum_scatter(
            totals[0].astype(jnp.bfloat16), "dp", scatter_dimension=1, tiled=True
        ).astype(jnp.float32),
        lax.psum_scatter(
            totals[1].astype(jnp.bfloat16), "dp", scatter_dimension=1, tiled=True
        ).astype(jnp.float32),
        lax.psum_scatter(
            totals[2].astype(jnp.bfloat16), "dp", scatter_dimension=1, tiled=True
        ).astype(jnp.float32),
        lax.psum_scatter(
            totals[3].astype(jnp.bfloat16), "dp", scatter_dimension=1, tiled=True
        ).astype(jnp.float32),
        lax.psum_scatter(
            totals[4].astype(jnp.bfloat16), "dp", scatter_dimension=1, tiled=True
        ).astype(jnp.float32),
        lax.psum_scatter(
            totals[5].astype(jnp.bfloat16), "dp", scatter_dimension=1, tiled=True
        ).astype(jnp.float32),
        lax.psum_scatter(
            totals[6].astype(jnp.bfloat16), "dp", scatter_dimension=0, tiled=True
        ).astype(jnp.float32),
        lax.psum_scatter(
            totals[7].astype(jnp.bfloat16), "dp", scatter_dimension=1, tiled=True
        ).astype(jnp.float32),
        lax.psum_scatter(
            tiled_scales.astype(jnp.bfloat16), "dp", scatter_dimension=0, tiled=True
        ).astype(jnp.float32),
    )
    return (
        section_out.reshape(1, micro_count * pack_rows, model_width),
        input_grads.reshape(1, micro_count * pack_rows, model_width),
        totals[0][None],
        totals[1][None],
        totals[2][None],
        totals[3][None],
        totals[4][None],
        totals[5][None],
        totals[6][None],
        totals[7][None],
        totals[8][None],
    )


def solution(mesh):
    return jax.shard_map(
        body,
        mesh=mesh,
        in_specs=(
            P("dp", None),
            P("dp", None),
            P("dp"),
            P("dp"),
            P("pipe", None, "dp"),
            P("pipe", None, "dp"),
            P("pipe", None, "dp"),
            P("pipe", None, "dp"),
            P("pipe", None, "dp"),
            P("pipe", None, "dp"),
            P("pipe", "dp"),
            P("pipe", None, "dp"),
            P("pipe", None),
        ),
        out_specs=(
            P("pipe", "dp", None),
            P("pipe", "dp", None),
            P("pipe", None, "dp"),
            P("pipe", None, "dp"),
            P("pipe", None, "dp"),
            P("pipe", None, "dp"),
            P("pipe", None, "dp"),
            P("pipe", None, "dp"),
            P("pipe", "dp"),
            P("pipe", None, "dp"),
            P("pipe", None),
        ),
        check_vma=False,
    )
```

profile of v0, /device:TPU:0, one launch (start us, length us, event | category | flops | bytes accessed | tf_op | source)
XLA Modules:
  0.0 1419.6 jit_solution(4110561430873941045)
XLA Ops:
  10.8 26.4 %all-gather = bf16[1,3,1024]{1,0,2:T(2,128)(2,1)S(1)} all-gather(bf16[1,3,32]{1,0,2:T(2,128)(2,1)S(1)} %copy.536), channel_id=2, replica_groups=mesh['pipe'=4,'dp'=32] {'dp'}, dimensions={2}, use_global_device_ids=true | all-gather | bytes 6336 | tf_op jit(solution)/shard_map/all_gather | solution.py:259
  38.3 24.2 %all-gather.1 = bf16[1,7,1024]{1,0,2:T(2,128)(2,1)S(1)} all-gather(bf16[1,7,32]{1,0,2:T(2,128)(2,1)S(1)} %copy.538), channel_id=3, replica_groups=mesh['pipe'=4,'dp'=32] {'dp'}, dimensions={2}, use_global_device_ids=true | all-gather | bytes 14784 | tf_op jit(solution)/shard_map/all_gather | solution.py:260
  63.6 19.1 %all-gather.6 = bf16[1,4096]{1,0:T(2,128)(2,1)S(1)} all-gather(bf16[1,128]{1,0:T(2,128)(2,1)} %param.43), channel_id=8, replica_groups=mesh['pipe'=4,'dp'=32] {'dp'}, dimensions={1}, use_global_device_ids=true | all-gather | bytes 8448 | tf_op jit(solution)/shard_map/all_gather | solution.py:261
  82.7 20.4 %all-gather.5 = bf16[1,2,4096]{2,1,0:T(2,128)(2,1)S(1)} all-gather(bf16[1,2,128]{2,1,0:T(2,128)(2,1)} %param.44), channel_id=7, replica_groups=mesh['pipe'=4,'dp'=32] {'dp'}, dimensions={2}, use_global_device_ids=true | all-gather | bytes 16896 | tf_op jit(solution)/shard_map/all_gather | solution.py:262
  108.0 60.7 %all-gather.17.cloned.1.call-done = bf16[1,1024,4096]{2,1,0:T(8,128)(2,1)} async-done(((bf16[1,1024,128]{2,1,0:T(8,128)(2,1)}), bf16[1,1024,4096]{2,1,0:T(8,128)(2,1)}) %all-gather.17.cloned.1.call-update) | async-done | bytes 8388624 | tf_op jit(solution)/shard_map/all_gather | solution.py:257
  168.6 54.8 %all-gather.19.cloned.1.call-done = bf16[1,4096,1024]{1,2,0:T(8,128)(2,1)} async-done(((bf16[1,4096,32]{1,2,0:T(8,128)(2,1)}), bf16[1,4096,1024]{1,2,0:T(8,128)(2,1)}) %all-gather.19.cloned.1.call-update) | async-done | bytes 8388624 | tf_op jit(solution)/shard_map/all_gather | solution.py:258
  223.4 22.9 %conditional.10 = (bf16[64,1024]{1,0:T(8,128)(2,1)S(1)}) conditional(s32[]{:T(128)} %convert_element_type.1230, bf16[64,1024]{1,0:T(8,128)(2,1)S(1)} %get-tuple-element.2666, (bf16[64,1024]{1,0:T(8,128)(2,1)S(1)}, bf16[3,1024]{1,0:T(4,128)(2,1)S(1)}, bf16[7,1024]{1,0:T(8,128)(2,1)S(1)}, bf16[1024,3072]{0,1:T(8,128)(2,1)}, s32[2,64]{1,0:T(2,128)S(1)}, ...), branch_computations={%region_0.1_spmd, %region_1.12_spmd} | conditional | flops 1635405184 | bytes 69138616 | solution.py:282
  237.8 5.4 fusion.507
  252.0 25.3 %conditional.11 = (bf16[64,1024]{1,0:T(8,128)(2,1)S(1)}) conditional(s32[]{:T(128)} %convert_element_type.1231, bf16[64,1024]{1,0:T(8,128)(2,1)S(1)} %get-tuple-element.2399, (bf16[64,1024]{1,0:T(8,128)(2,1)S(1)}, bf16[3,1024]{1,0:T(4,128)(2,1)S(1)}, bf16[7,1024]{1,0:T(8,128)(2,1)S(1)}, bf16[1024,3072]{0,1:T(8,128)(2,1)}, s32[2,64]{1,0:T(2,128)S(1)}, ...), branch_computations={%region_12.13_spmd, %region_13.24_spmd} | conditional | flops 1635405184 | bytes 69138616 | solution.py:282
  268.9 5.4 fusion.514
  284.5 29.7 %collective-permute-start.2 = (bf16[64,1024]{1,0:T(8,128)(2,1)S(1)}, bf16[64,1024]{1,0:T(8,128)(2,1)S(1)}, u32[]{:S(2)}, u32[]{:S(2)}) collective-permute-start(bf16[64,1024]{1,0:T(8,128)(2,1)S(1)} %get-tuple-element.2771), channel_id=1, source_target_pairs={{0,32},{32,64},{64,96},{1,33},{33,65},{65,97},{2,34},{34,66},{66,9... | collective-permute-start | bytes 393224 | tf_op jit(solution)/shard_map/ppermute | solution.py:12
  324.6 30.8 %conditional.15 = (bf16[64,1024]{1,0:T(8,128)(2,1)}, f32[1024,4096]{1,0:T(8,128)}, f32[3,1024]{1,0:T(4,128)}, f32[7,1024]{1,0:T(8,128)}, f32[4096]{0:T(1024)}, /...) conditional(s32[]{:T(128)} %convert_element_type.1235, ...), branch_computations={%region_60.61_spmd, %region_61.95_spmd} | conditional | flops 4381684736 | bytes 198079408 | solution.py:322
  325.3 7.8 broadcast_in_dim.822
  335.5 6.1 broadcast_in_dim.820.clone
  344.0 7.8 broadcast_in_dim.823.clone
  357.2 29.3 %collective-permute-done.4 = bf16[64,1024]{1,0:T(8,128)(2,1)S(1)} collective-permute-done((bf16[64,1024]{1,0:T(8,128)(2,1)}, bf16[64,1024]{1,0:T(8,128)(2,1)S(1)}, u32[]{:S(2)}, u32[]{:S(2)}) %collective-permute-start.4) | collective-permute-done | bytes 131104 | tf_op jit(solution)/shard_map/ppermute | solution.py:12
  387.2 30.6 %conditional.16 = (bf16[64,1024]{1,0:T(8,128)(2,1)}, f32[1024,4096]{1,0:T(8,128)}, f32[3,1024]{1,0:T(4,128)}, f32[7,1024]{1,0:T(8,128)}, f32[4096]{0:T(1024)}, /...) conditional(s32[]{:T(128)} %convert_element_type.1236, ...), branch_computations={%region_95.96_spmd, %region_96.130_spmd} | conditional | flops 4381684736 | bytes 198339472 | solution.py:322
  387.9 7.8 broadcast_in_dim.842
  398.1 6.1 broadcast_in_dim.840.clone
  406.7 7.8 broadcast_in_dim.843.clone
  419.6 6.2 collective-permute-done.5
  425.8 30.5 %conditional.17 = (bf16[64,1024]{1,0:T(8,128)(2,1)}, f32[1024,4096]{1,0:T(8,128)}, f32[3,1024]{1,0:T(4,128)S(1)}, f32[7,1024]{1,0:T(8,128)}, f32[4096]{0:T(1024)...) conditional(s32[]{:T(128)} %convert_element_type.1237, ...), branch_computations={%region_130.131_spmd, %region_131.165_spmd} | conditional | flops 4381684736 | bytes 198388656 | solution.py:322
  426.5 7.9 broadcast_in_dim.862
  436.2 6.1 broadcast_in_dim.860.clone
  444.9 7.9 broadcast_in_dim.863.clone
  458.8 171.4 %collective-permute-done.6 = bf16[64,1024]{1,0:T(8,128)(2,1)S(1)} collective-permute-done((bf16[64,1024]{1,0:T(8,128)(2,1)}, bf16[64,1024]{1,0:T(8,128)(2,1)S(1)}, u32[]{:S(2)}, u32[]{:S(2)}) %collective-permute-start.6) | collective-permute-done | bytes 131104 | tf_op jit(solution)/shard_map/ppermute | solution.py:12
  630.1 86.6 %conditional.18 = (bf16[64,1024]{1,0:T(8,128)(2,1)}, f32[1024,4096]{1,0:T(8,128)}, f32[3,1024]{1,0:T(4,128)S(1)}, f32[7,1024]{1,0:T(8,128)}, f32[4096]{0:T(1024)...) conditional(s32[]{:T(128)} %convert_element_type.1238, ...), branch_computations={%region_165.166_spmd, %region_166.200_spmd} | conditional | flops 4381684736 | bytes 198388656 | solution.py:322
  652.3 5.4 fusion.401
  685.3 8.2 fusion.400
  698.3 7.1 fusion.395
  708.2 8.1 fusion.365
  719.2 6.5 collective-permute-done.7
  725.8 84.9 %conditional.19 = (bf16[64,1024]{1,0:T(8,128)(2,1)S(1)}, f32[1024,4096]{1,0:T(8,128)}, f32[3,1024]{1,0:T(4,128)}, f32[7,1024]{1,0:T(8,128)}, f32[4096]{0:T(1024)...) conditional(s32[]{:T(128)} %convert_element_type.1239, ...), branch_computations={%region_200.201_spmd, %region_201.235_spmd} | conditional | flops 4381684736 | bytes 198747408 | solution.py:322
  746.6 5.7 fusion.454
  779.5 8.2 fusion.453
  792.3 7.0 fusion.448
  802.1 8.1 fusion.418
  816.6 10.7 add_convert_fusion.58
  827.3 24.4 %add_convert_fusion.57 = bf16[1024,3072]{0,1:T(8,128)(2,1)} fusion(f32[1024,3072]{0,1:T(8,128)} %get-tuple-element.2227, f32[1024,3072]{0,1:T(8,128)} %get-tuple-element.2224, f32[1024,3072]{0,1:T(8,128)} %get-tuple-element.2221, f32[1024,3072]{0,1:T(8,128)} %get-tuple-element.2215, f32[1024,3072]{0,1:T(8,128)} %get-tuple-element.2218), kind=kLoop, calls=%fused_computation.907 | loop fusion | flops 15728640 | bytes 69206016 | tf_op jit(solution)/shard_map/convert_element_type | solution.py:331
  851.8 30.6 %add_convert_fusion.56 = bf16[1024,4096]{1,0:T(8,128)(2,1)} fusion(f32[1024,4096]{1,0:T(8,128)} %get-tuple-element.1824, f32[1024,4096]{1,0:T(8,128)} %get-tuple-element.1823, f32[1024,4096]{1,0:T(8,128)} %get-tuple-element.1822, f32[1024,4096]{1,0:T(8,128)} %get-tuple-element.1820, f32[1024,4096]{1,0:T(8,128)} %get-tuple-element.1821), kind=kLoop, calls=%fused_computation.906 | loop fusion | flops 20971520 | bytes 92274688 | tf_op jit(solution)/shard_map/convert_element_type | solution.py:337
  882.4 12.0 copy.667
  894.4 31.0 %add_convert_fusion.55 = bf16[4096,1024]{0,1:T(8,128)(2,1)} fusion(f32[4096,1024]{0,1:T(8,128)} %get-tuple-element.2229, f32[4096,1024]{0,1:T(8,128)} %get-tuple-element.2226, f32[4096,1024]{0,1:T(8,128)} %get-tuple-element.2223, f32[4096,1024]{0,1:T(8,128)} %get-tuple-element.2217, f32[4096,1024]{0,1:T(8,128)} %get-tuple-element.2220), kind=kLoop, calls=%fused_computation.905 | loop fusion | flops 20971520 | bytes 92274688 | tf_op jit(solution)/shard_map/convert_element_type | solution.py:340
  932.6 64.7 %all-reduce.2 = (bf16[4096]{0:T(1024)(128)(2,1)S(1)}, bf16[512]{0:T(512)(128)(2,1)S(1)}) all-reduce(bf16[4096]{0:T(1024)(128)(2,1)S(1)} %add_convert_fusion.61, bf16[512]{0:T(512)(128)(2,1)S(1)} %convert_element_type.1249), channel_id=16, replica_groups=mesh['pipe'=4,'dp'=32] {'dp'}, use_global_device_ids=true, to_apply=%region_241.242.clone | all-reduce | flops 4608 | bytes 18432
  1002.2 45.0 %reduce-scatter.28.cloned.1.call-done = bf16[128,2]{1,0:T(8,128)(2,1)} async-done(((bf16[4096,2]{1,0:T(8,128)(2,1)}), bf16[128,2]{1,0:T(8,128)(2,1)}) %reduce-scatter.28.cloned.1.call-update) | async-done | bytes 528
  1048.6 80.7 %reduce-scatter.18.cloned.1.call-done = bf16[1024,32]{0,1:T(8,128)(2,1)} async-done(((bf16[1024,1024]{0,1:T(8,128)(2,1)}), bf16[1024,32]{0,1:T(8,128)(2,1)}) %reduce-scatter.18.cloned.1.call-update) | async-done | bytes 65552 | tf_op jit(solution)/shard_map/reduce_scatter | solution.py:333
  1130.9 88.3 %reduce-scatter.16.cloned.1.call-done = bf16[1024,96]{0,1:T(8,128)(2,1)} async-done(((bf16[1024,3072]{0,1:T(8,128)(2,1)}), bf16[1024,96]{0,1:T(8,128)(2,1)}) %reduce-scatter.16.cloned.1.call-update) | async-done | bytes 196624 | tf_op jit(solution)/shard_map/reduce_scatter | solution.py:330
  1220.9 94.0 %reduce-scatter.22.cloned.1.call-done = bf16[128,1024]{1,0:T(8,128)(2,1)} async-done(((bf16[4096,1024]{1,0:T(8,128)(2,1)}), bf16[128,1024]{1,0:T(8,128)(2,1)}) %reduce-scatter.22.cloned.1.call-update) | async-done | bytes 262160
  1316.8 94.3 %reduce-scatter.20.cloned.1.call-done = bf16[4096,32]{0,1:T(8,128)(2,1)} async-done(((bf16[4096,1024]{0,1:T(8,128)(2,1)}), bf16[4096,32]{0,1:T(8,128)(2,1)}) %reduce-scatter.20.cloned.1.call-update) | async-done | bytes 262160 | tf_op jit(solution)/shard_map/reduce_scatter | solution.py:339
  (576 shorter events, 232.5 us)
Async XLA Ops:
  7.2 97.6 %all-gather.15.cloned.1.call-start = ((), (), s32[]{:S(2)}) async-start(), calls=%async_computation.11 | async-start | bytes 2162688 | tf_op jit(solution)/shard_map/all_gather | solution.py:256
  7.9 100.0 %all-gather.13.cloned.1.call-start = ((), (), s32[]{:S(2)}) async-start(), calls=%async_computation.10 | async-start | bytes 6488064 | tf_op jit(solution)/shard_map/all_gather | solution.py:255
  8.7 160.0 %all-gather.17.cloned.1.call-start = ((), (), s32[]{:S(2)}) async-start(), calls=%async_computation.12 | async-start | bytes 8650752 | tf_op jit(solution)/shard_map/all_gather | solution.py:257
  9.4 214.0 %all-gather.19.cloned.1.call-start = ((), (), s32[]{:S(2)}) async-start(), calls=%async_computation.13 | async-start | bytes 8650752 | tf_op jit(solution)/shard_map/all_gather | solution.py:258
  10.0 989.5 %reduce-scatter.24.cloned.1.call-start = ((), (), s32[]{:S(2)}) async-start(), calls=%async_computation.15 | async-start | bytes 270336
  63.5 261.0 %copy-start.226 = (s32[2,64]{1,0:T(2,128)}, s32[2,64]{1,0:T(2,128)S(1)}, u32[]{:S(2)}) copy-start(s32[2,64]{1,0:T(2,128)S(1)} %reshape.1488) | copy-start | bytes 1540
  223.4 27.7 %copy-start.76 = (bf16[128,1024]{1,0:T(8,128)(2,1)S(1)}, bf16[128,1024]{1,0:T(8,128)(2,1)}, u32[]{:S(2)}) copy-start(bf16[128,1024]{1,0:T(8,128)(2,1)} %param.33) | copy-start | bytes 786436
  223.4 12.9 copy-start.1
  246.3 4.7 collective-permute-start
  252.1 14.3 %copy-start.2 = (bf16[1024,1024]{0,1:T(8,128)(2,1)S(1)}, bf16[1024,1024]{0,1:T(8,128)(2,1)}, u32[]{:S(2)}) copy-start(bf16[1024,1024]{0,1:T(8,128)(2,1)} %get-tuple-element.2067) | copy-start | bytes 6291460 | tf_op jit(solution)/shard_map/cond
  277.3 7.1 collective-permute-start.1
  284.5 32.2 %collective-permute-start.2 = (bf16[64,1024]{1,0:T(8,128)(2,1)S(1)}, bf16[64,1024]{1,0:T(8,128)(2,1)S(1)}, u32[]{:S(2)}, u32[]{:S(2)}) collective-permute-start(bf16[64,1024]{1,0:T(8,128)(2,1)S(1)} %get-tuple-element.2771), channel_id=1, source_target_pairs={{0,32},{32,64},{64,96},{1,33},{33,65},{65,97},{2,34},{34,66},{66,9... | collective-permute-start | bytes 393224 | tf_op jit(solution)/shard_map/ppermute | solution.py:12
  316.9 6.9 collective-permute-start.3
  355.9 30.6 %collective-permute-start.4 = (bf16[64,1024]{1,0:T(8,128)(2,1)}, bf16[64,1024]{1,0:T(8,128)(2,1)S(1)}, u32[]{:S(2)}, u32[]{:S(2)}) collective-permute-start(bf16[64,1024]{1,0:T(8,128)(2,1)} %get-tuple-element.1805), channel_id=1, source_target_pairs={{32,0},{64,32},{96,64},{33,1},{65,33},{97,65},{34,2},{66,34},{98,6... | collective-permute-start | bytes 393224 | tf_op jit(solution)/shard_map/ppermute | solution.py:12
  418.3 7.5 collective-permute-start.5
  457.5 172.7 %collective-permute-start.6 = (bf16[64,1024]{1,0:T(8,128)(2,1)}, bf16[64,1024]{1,0:T(8,128)(2,1)S(1)}, u32[]{:S(2)}, u32[]{:S(2)}) collective-permute-start(bf16[64,1024]{1,0:T(8,128)(2,1)} %get-tuple-element.1807), channel_id=1, source_target_pairs={{32,0},{64,32},{96,64},{33,1},{65,33},{97,65},{34,2},{66,34},{98,6... | collective-permute-start | bytes 393224 | tf_op jit(solution)/shard_map/ppermute | solution.py:12
  630.3 12.6 copy-start.231
  630.3 18.0 %copy-start.8 = (bf16[1024,1024]{0,1:T(8,128)(2,1)S(1)}, bf16[1024,1024]{0,1:T(8,128)(2,1)}, u32[]{:S(2)}) copy-start(bf16[1024,1024]{0,1:T(8,128)(2,1)} %get-tuple-element.2182) | copy-start | bytes 6291460 | tf_op jit(solution)/shard_map/cond
  630.9 19.4 %copy-start.124 = (f32[1,1024]{1,0:T(1,128)}, f32[1,1024]{1,0:T(1,128)S(1)}, u32[]{:S(2)}) copy-start(f32[1,1024]{1,0:T(1,128)S(1)} %get-tuple-element.2632) | copy-start | bytes 12292 | tf_op jit(solution)/shard_map/cond
  630.9 21.3 %copy-start.100 = (f32[1,1024]{1,0:T(1,128)}, f32[1,1024]{1,0:T(1,128)S(1)}, u32[]{:S(2)}) copy-start(f32[1,1024]{1,0:T(1,128)S(1)} %get-tuple-element.2608) | copy-start | bytes 12292 | tf_op jit(solution)/shard_map/cond
  644.3 13.5 copy-start.129
  651.4 15.4 %copy-start.16 = (f32[64,1024]{1,0:T(8,128)}, f32[64,1024]{1,0:T(8,128)S(1)}, u32[]{:S(2)}) copy-start(f32[64,1024]{1,0:T(8,128)S(1)} %get-tuple-element.2376) | copy-start | bytes 786436 | tf_op jit(solution)/shard_map/cond
  651.4 15.3 %copy-start.145 = (f32[64]{0:T(128)}, f32[64]{0:T(128)S(1)}, u32[]{:S(2)}) copy-start(f32[64]{0:T(128)S(1)} %broadcast_multiply_fusion.33) | copy-start | bytes 772 | tf_op jit(solution)/shard_map/cond
  651.6 15.1 %copy-start.155 = (f32[64]{0:T(128)}, f32[64]{0:T(128)S(1)}, u32[]{:S(2)}) copy-start(f32[64]{0:T(128)S(1)} %fusion.392) | copy-start | bytes 772 | tf_op jit(solution)/shard_map/cond
  671.6 12.6 copy-start.212
  671.6 12.6 copy-start.138
  671.6 12.6 copy-start.166
  671.6 12.9 copy-start.49
  673.3 12.0 copy-start.17
  717.9 7.8 collective-permute-start.7
  725.9 12.8 copy-start.232
  725.9 18.1 %copy-start.9 = (bf16[1024,1024]{0,1:T(8,128)(2,1)S(1)}, bf16[1024,1024]{0,1:T(8,128)(2,1)}, u32[]{:S(2)}) copy-start(bf16[1024,1024]{0,1:T(8,128)(2,1)} %get-tuple-element.2201) | copy-start | bytes 6291460 | tf_op jit(solution)/shard_map/cond
  732.2 13.9 copy-start.180
  746.3 14.4 %copy-start.18 = (f32[64,1024]{1,0:T(8,128)}, f32[64,1024]{1,0:T(8,128)S(1)}, u32[]{:S(2)}) copy-start(f32[64,1024]{1,0:T(8,128)S(1)} %get-tuple-element.2391) | copy-start | bytes 786436 | tf_op jit(solution)/shard_map/cond
  746.3 14.4 %copy-start.147 = (f32[64]{0:T(128)}, f32[64]{0:T(128)S(1)}, u32[]{:S(2)}) copy-start(f32[64]{0:T(128)S(1)} %broadcast_multiply_fusion.37) | copy-start | bytes 772 | tf_op jit(solution)/shard_map/cond
  746.5 14.2 %copy-start.157 = (f32[64]{0:T(128)}, f32[64]{0:T(128)S(1)}, u32[]{:S(2)}) copy-start(f32[64]{0:T(128)S(1)} %fusion.445) | copy-start | bytes 772 | tf_op jit(solution)/shard_map/cond
  765.7 12.6 copy-start.214
  765.7 12.6 copy-start.168
  765.7 12.9 copy-start.51
  810.6 16.6 %copy-start.93 = (bf16[64,1024]{1,0:T(8,128)(2,1)}, bf16[64,1024]{1,0:T(8,128)(2,1)S(1)}, u32[]{:S(2)}) copy-start(bf16[64,1024]{1,0:T(8,128)(2,1)S(1)} %get-tuple-element.1809) | copy-start | bytes 393220
  812.4 188.5 %reduce-scatter.26.cloned.1.call-start = ((), (), s32[]{:S(2)}) async-start(), calls=%async_computation.16 | async-start | bytes 270336
  814.2 233.1 %reduce-scatter.28.cloned.1.call-start = ((), (), s32[]{:S(2)}) async-start(), calls=%async_computation.17 | async-start | bytes 1081344
  816.5 312.9 %reduce-scatter.18.cloned.1.call-start = ((), (), s32[]{:S(2)}) async-start(), calls=%async_computation.8 | async-start | bytes 2162688 | tf_op jit(solution)/shard_map/reduce_scatter | solution.py:333
  827.3 391.9 %reduce-scatter.16.cloned.1.call-start = ((), (), s32[]{:S(2)}) async-start(), calls=%async_computation.7 | async-start | bytes 6488064 | tf_op jit(solution)/shard_map/reduce_scatter | solution.py:330
  851.7 463.1 %reduce-scatter.22.cloned.1.call-start = ((), (), s32[]{:S(2)}) async-start(), calls=%async_computation.14 | async-start | bytes 8650752
  894.4 516.7 %reduce-scatter.20.cloned.1.call-start = ((), (), s32[]{:S(2)}) async-start(), calls=%async_computation.9 | async-start | bytes 8650752 | tf_op jit(solution)/shard_map/reduce_scatter | solution.py:339
  929.9 483.0 %copy-start.55 = (bf16[2,64,1024]{2,1,0:T(8,128)(2,1)}, bf16[2,64,1024]{2,1,0:T(8,128)(2,1)S(1)}, u32[]{:S(2)}) copy-start(bf16[2,64,1024]{2,1,0:T(8,128)(2,1)S(1)} %bitcast_dynamic-update-slice_fusion.9) | copy-start | bytes 786436
  999.4 413.5 %copy-start.52 = (bf16[2,64,1024]{2,1,0:T(8,128)(2,1)}, bf16[2,64,1024]{2,1,0:T(8,128)(2,1)S(1)}, u32[]{:S(2)}) copy-start(bf16[2,64,1024]{2,1,0:T(8,128)(2,1)S(1)} %bitcast_dynamic-update-slice_fusion) | copy-start | bytes 786436
  (89 other events, 566.4 us)
Sparse Core Ops, SparseCore 0:
  10.3 46.7 all-gather.14
  59.4 48.5 all-gather.12
  110.1 58.4 all-gather.16
  170.7 52.6 all-gather.18
  812.5 74.1 reduce-scatter.23
  890.5 76.2 reduce-scatter.25
  970.3 76.9 reduce-scatter.27
  1051.2 78.1 reduce-scatter.17
  1133.6 85.5 reduce-scatter.15
  1222.7 92.0 reduce-scatter.21
  1319.0 92.0 reduce-scatter.19
where the time goes:
time: 1430 us; the launch traced here: 1420 us
  waiting for transfers between devices  747 us (52%)
  blocking collectives  155 us (11%)
  matrix products  154 us (11%)
  other arithmetic  150 us (10%)
  local copies, waits for them, and re-layouts  139 us (10%)
  starting transfers between devices  45.8 us (3%)
  between operations  16 us (1%)
    ppermute x8, waiting for transfers between devices, passed_along(): return lax.ppermute(value, axis, pairs)  223 us
    unnamed x15, waiting for transfers between devices  142 us
    reduce_scatter x1, waiting for transfers between devices, body(): lax.psum_scatter(totals[3].astype(jnp.bfloat16), 'dp', scatter_dimension=...  94.3 us
    reduce_scatter x1, waiting for transfers between devices, body(): lax.psum_scatter(totals[0].astype(jnp.bfloat16), 'dp', scatter_dimension=...  88.3 us
    reduce_scatter x1, waiting for transfers between devices, body(): lax.psum_scatter(totals[1].astype(jnp.bfloat16), 'dp', scatter_dimension=...  80.7 us
    broadcast_in_dim x24, local copies, waits for them, and re-layouts, body(): jnp.zeros(p.shape, jnp.float32)  79.6 us
    unnamed x1, blocking collectives  64.7 us
    all_gather x1, waiting for transfers between devices, body(): lax.all_gather(feed_up[0], 'dp', axis=1, tiled=True)  60.7 us
  transfers between devices with their start and end apart: 19, of which 16 were waited for; matrix products, arithmetic and copies ran while one was open for 9% of the time, Pallas kernels for 0%

commit v1 on v0

v1 whole, which is shorter than its diff:
```python
import functools

import jax
import jax.numpy as jnp
from jax import lax
from jax.experimental import pallas as pl
from jax.experimental.pallas import tpu as pltpu
from jax.sharding import PartitionSpec as P

MESH = pl.DeviceIdType.MESH
EPS = 1e-05
F32, BF16 = jnp.float32, jnp.bfloat16
VMEM_LIMIT = 60 * 1024 * 1024

S, A, B, C, D = range(5)
ROWS = (16, 96, 32, 128, 32)
COLS = (128, 1024, 1024, 1024, 4096)
TYPES = (F32, BF16, BF16, BF16, BF16)
TOK, WIDTH, FF, QKV = 128, 1024, 4096, 3072
OFFS = (0, 3, 1, 2)


class Place:
    def __init__(self):
        self.s = lax.axis_index("pipe")
        d = lax.axis_index("dp")
        self.d = d
        self.c = d % 2
        y, z = (d // 2) % 4, d // 8
        self.f = y + self.c * (z - y)
        self.g = z + self.c * (y - z)
        self.sf = 2 + 6 * self.c
        self.sg = 8 - 6 * self.c
        self.sib = d + 1 - 2 * self.c

    def dp(self, of, og):
        return ((self.f + of) % 4) * self.sf + ((self.g + og) % 4) * self.sg + self.c

    def sib_dp(self, of, og):
        return ((self.g + of) % 4) * self.sg + ((self.f + og) % 4) * self.sf + 1 - self.c

    def barrier(self, along_pipe):
        sem = pltpu.get_barrier_semaphore()
        near = [self.dp(1, 0), self.dp(3, 0), self.dp(0, 1), self.dp(0, 3), self.sib]
        for to in near:
            pl.semaphore_signal(sem, inc=1, device_id=(self.s, to), device_id_type=MESH)
        if along_pipe:
            for by in (1, 3):
                pl.semaphore_signal(sem, inc=1, device_id=((self.s + by) % 4, self.d), device_id_type=MESH)
        pl.semaphore_wait(sem, 7 if along_pipe else 5)


def part(ref, rows, d, half):
    if half is None:
        return ref.at[pl.ds(pl.multiple_of(d * rows, rows), rows)]
    h = rows // 2
    return ref.at[pl.ds(pl.multiple_of(d * rows + half * h, h), h)]


def remote(src, dst, send, recv, s, to):
    return pltpu.make_async_remote_copy(
        src_ref=src, dst_ref=dst, send_sem=send, recv_sem=recv, device_id=(s, to), device_id_type=MESH
    )


class Gather:
    def __init__(self, place, bufs, send, recv):
        self.p, self.bufs, self.send, self.recv = place, bufs, send, recv
        self.open = []

    def put(self, k, slot, d, half, to):
        ref = part(self.bufs[k], ROWS[k], d, half)
        copy = remote(ref, ref, self.send.at[k, slot], self.recv.at[k, slot], self.p.s, to)
        copy.start()
        self.open.append(copy)

    def got(self, k, slot, d, half):
        ref = part(self.bufs[k], ROWS[k], d, half)
        remote(ref, ref, self.send.at[k, slot], self.recv.at[k, slot], self.p.s, self.p.sib).wait_recv()

    def spread(self, k, j):
        p = self.p
        d = p.dp(OFFS[j], 0)
        self.put(k, 4 + 4 * j, d, None, p.dp(0, 1))
        self.put(k, 5 + 4 * j, d, None, p.dp(0, 3))
        self.put(k, 20 + 4 * j, d, None, p.sib)

    def first(self, k):
        p = self.p
        self.put(k, 0, p.d, None, p.dp(1, 0))
        self.put(k, 1, p.d, None, p.dp(3, 0))
        self.spread(k, 0)

    def ring(self, k):
        p = self.p
        left, right = p.dp(3, 0), p.dp(1, 0)
        self.got(k, 0, left, None)
        self.put(k, 2, left, 0, right)
        self.spread(k, 1)
        self.got(k, 1, right, None)
        self.put(k, 3, right, 1, left)
        self.spread(k, 2)

    def far(self, k):
        d = self.p.dp(2, 0)
        self.got(k, 2, d, 0)
        self.got(k, 3, d, 1)
        self.spread(k, 3)

    def second(self, k):
        p = self.p
        for j in range(4):
            low, high = p.dp(OFFS[j], 3), p.dp(OFFS[j], 1)
            self.got(k, 4 + 4 * j, low, None)
            self.put(k, 6 + 4 * j, low, 0, p.dp(0, 1))
            self.put(k, 21 + 4 * j, low, None, p.sib)
            self.got(k, 5 + 4 * j, high, None)
            self.put(k, 7 + 4 * j, high, 1, p.dp(0, 3))
            self.put(k, 22 + 4 * j, high, None, p.sib)

    def last(self, k):
        p = self.p
        for j in range(4):
            d = p.dp(OFFS[j], 2)
            self.got(k, 6 + 4 * j, d, 0)
            self.got(k, 7 + 4 * j, d, 1)
            self.put(k, 23 + 4 * j, d, None, p.sib)

    def whole(self, k):
        for j in range(4):
            for i in range(4):
                self.got(k, 20 + 4 * j + i, self.p.sib_dp(OFFS[j], OFFS[i]), None)

    def close(self):
        for copy in self.open:
            copy.wait_send()

    def run(self, order):
        n = len(order)
        for t in range(n + 2):
            if t == 0:
                self.first(order[0])
            if t + 1 < n:
                self.first(order[t + 1])
            if t < n:
                self.ring(order[t])
            if 0 <= t - 1 < n:
                self.far(order[t - 1])
                self.second(order[t - 1])
            if 0 <= t - 2 < n:
                self.last(order[t - 2])


def dot(a, b, ca, cb):
    return lax.dot_general(a, b, (((ca,), (cb,)), ((), ())), preferred_element_type=F32)


def centered(x):
    c = x - jnp.mean(x, axis=-1, keepdims=True)
    r = lax.rsqrt(jnp.mean(c * c, axis=-1, keepdims=True) + EPS)
    return c, r


def norm(x, gain, bias):
    c, r = centered(x)
    return c * r * gain + bias


def norm_back(x, gain, gy):
    c, r = centered(x)
    hat = c * r
    gh = gy * gain
    gx = r * (gh - jnp.mean(gh, axis=-1, keepdims=True) - hat * jnp.mean(gh * hat, axis=-1, keepdims=True))
    return gx, gy * hat


def rows_of(i, n):
    return pl.ds(pl.multiple_of(i * n, n), n)


def col_sum(x):
    return jnp.sum(x, axis=0, keepdims=True)


K0, K1 = 0.7978845608028654, 0.044715


def gelu(x):
    return 0.5 * x * (1.0 + jnp.tanh(K0 * (x + K1 * x * x * x)))


def gelu_both(x):
    t = jnp.tanh(K0 * (x + K1 * x * x * x))
    u = 0.5 * x * (1.0 + t)
    du = 0.5 * (1.0 + t) + 0.5 * x * (1.0 - t * t) * K0 * (1.0 + 3.0 * K1 * x * x)
    return u, du


def head_masks():
    lane = lax.broadcasted_iota(jnp.int32, (1, 128), 1)
    even = jnp.where(lane < 64, 1.0, 0.0)
    return even.astype(BF16), (1.0 - even).astype(BF16)


def two_rows(x, even, odd):
    return jnp.concatenate([x * even, x * odd], axis=0)


def matmul_loop(width, tile, unroll=1):
    def run(body):
        def step(i, carry):
            body(pl.ds(pl.multiple_of(i * tile, tile), tile))
            return carry

        lax.fori_loop(0, width // tile, step, 0, unroll=unroll)

    return run


def each(count, unroll=1):
    def run(body):
        def step(i, carry):
            body(i)
            return carry

        lax.fori_loop(0, count, step, 0, unroll=unroll)

    return run


def forward(z_ref, w, pd, pm, hs_ref, segc_ref, segr_ref, keep, send_out):
    wa, wb, wc, wd = w

    @each(4)
    def _(i):
        r = rows_of(i, 32)
        keep["a1"][r, :] = norm(z_ref[r, :].astype(F32), pd[0:1, :], pd[3:4, :]).astype(BF16)

    a1 = keep["a1"]
    for third in range(3):
        bias_row = (4, None, 5)[third]

        @matmul_loop(WIDTH, 256, 2)
        def _(cols, third=third, bias_row=bias_row):
            at = pl.ds(pl.multiple_of(third * WIDTH + cols.start, 256), 256)
            acc = dot(a1[...], wa[at, :], 1, 1)
            if bias_row is not None:
                acc = acc + pd[bias_row : bias_row + 1, cols]
            keep["qkv"][:, at] = acc.astype(BF16)

    qkv = keep["qkv"]
    row = lax.broadcasted_iota(jnp.int32, (TOK, TOK), 0)
    col = lax.broadcasted_iota(jnp.int32, (TOK, TOK), 1)
    ok = (segc_ref[...] == segr_ref[...]) & (col <= row) & (row // 64 == col // 64)
    okf = jnp.where(ok, 1.0, 0.0)
    even, odd = head_masks()

    @each(8, 2)
    def _(p):
        cols = pl.ds(pl.multiple_of(p * 128, 128), 128)
        q = qkv[:, cols]
        k = qkv[:, pl.ds(pl.multiple_of(WIDTH + p * 128, 128), 128)]
        v = qkv[:, pl.ds(pl.multiple_of(2 * WIDTH + p * 128, 128), 128)]
        sc = dot(two_rows(q, even, odd), k, 1, 1) * 0.125
        okk = jnp.concatenate([okf, okf], axis=0) > 0.5
        sc = jnp.where(okk, sc, -1000000000.0)
        e = jnp.exp(sc - jnp.max(sc, axis=-1, keepdims=True))
        pr = e / jnp.sum(e, axis=-1, keepdims=True)
        keep["p"][rows_of(p, 256), :] = pr
        pb = pr.astype(BF16)
        both = jnp.concatenate([pb[:TOK], pb[TOK:]], axis=1)
        mixed = dot(both, two_rows(v, even, odd), 1, 0)
        keep["mixed"][:, cols] = mixed
        keep["scaled"][:, cols] = (mixed * hs_ref[:, cols]).astype(BF16)

    @matmul_loop(WIDTH, 256, 2)
    def _(cols):
        keep["attn"][:, cols] = dot(keep["scaled"][...], wb[cols, :], 1, 1) + pd[6:7, cols]

    @each(4)
    def _(i):
        r = rows_of(i, 32)
        z2 = z_ref[r, :].astype(F32) + norm(keep["attn"][r, :], pd[1:2, :], pd[7:8, :])
        keep["z2"][r, :] = z2
        keep["a2"][r, :] = norm(z2, pd[2:3, :], pd[8:9, :]).astype(BF16)

    @matmul_loop(FF, 256, 2)
    def _(cols):
        keep["hid"][:, cols] = dot(keep["a2"][...], wc[cols, :], 1, 1) + pm[11:12, cols]

    @each(8)
    def _(i):
        r = rows_of(i, 16)
        keep["mid"][r, :] = norm(gelu(keep["hid"][r, :]), pm[10:11, :], pm[12:13, :]).astype(BF16)

    for n in range(4):
        cols = slice(n * 256, (n + 1) * 256)
        acc = dot(keep["mid"][...], wd[cols, :], 1, 1)
        keep["out"][:, cols] = (keep["z2"][:, cols] + acc + pd[9:10, cols]).astype(BF16)
        send_out(n)


def backward(g_ref, w, pd, pm, hs_ref, kept, out, tmp, wait_w, send_out):
    wa, wb, wc, wd = w
    gd, gm = out["gd"], out["gm"]
    gd[...] = jnp.zeros_like(gd)
    gm[...] = jnp.zeros_like(gm)
    wait_w(D)

    @matmul_loop(FF, 256, 2)
    def _(cols):
        tmp["ff"][:, cols] = dot(g_ref[...], wd[:, cols], 1, 0)

    gd[9:10, :] = col_sum(g_ref[...].astype(F32))

    @each(8)
    def _(i):
        r = rows_of(i, 16)
        gmid = tmp["ff"][r, :]
        u, du = gelu_both(kept["hid"][r, :])
        gu, gg = norm_back(u, pm[10:11, :], gmid)
        gh = (gu * du).astype(BF16)
        out["ghid"][r, :] = gh
        gm[10:11, :] += col_sum(gg)
        gm[12:13, :] += col_sum(gmid)
        gm[11:12, :] += col_sum(gh.astype(F32))

    wait_w(C)

    @matmul_loop(WIDTH, 256, 1)
    def _(cols):
        tmp["w"][:, cols] = dot(out["ghid"][...], wc[:, cols], 1, 0)

    @each(4)
    def _(i):
        r = rows_of(i, 32)
        ga2 = tmp["w"][r, :]
        gz, gg = norm_back(kept["z2"][r, :], pd[2:3, :], ga2)
        gd[2:3, :] += col_sum(gg)
        gd[8:9, :] += col_sum(ga2)
        gz = gz + g_ref[r, :].astype(F32)
        tmp["gz2"][r, :] = gz
        gat, gg = norm_back(kept["attn"][r, :], pd[1:2, :], gz)
        gd[1:2, :] += col_sum(gg)
        gd[7:8, :] += col_sum(gz)
        gat = gat.astype(BF16)
        out["gattn"][r, :] = gat
        gd[6:7, :] += col_sum(gat.astype(F32))

    wait_w(B)
    even, odd = head_masks()

    @each(8, 2)
    def _(p):
        cols = pl.ds(pl.multiple_of(p * 128, 128), 128)
        kcols = pl.ds(pl.multiple_of(WIDTH + p * 128, 128), 128)
        vcols = pl.ds(pl.multiple_of(2 * WIDTH + p * 128, 128), 128)
        gs = dot(out["gattn"][...], wb[:, cols], 1, 0)
        tmp["hs"][:, cols] = col_sum(gs * kept["mixed"][:, cols])
        gmx = (gs * hs_ref[:, cols]).astype(BF16)
        q, k, v = kept["qkv"][:, cols], kept["qkv"][:, kcols], kept["qkv"][:, vcols]
        gmx2 = two_rows(gmx, even, odd)
        gp = dot(gmx2, v, 1, 1)
        pr = kept["p"][rows_of(p, 256), :]
        gsc = (pr * (gp - jnp.sum(pr * gp, axis=-1, keepdims=True))).astype(BF16)
        both = jnp.concatenate([gsc[:TOK], gsc[TOK:]], axis=1)
        gq = dot(both, two_rows(k, even, odd), 1, 0) * 0.125
        gk = dot(gsc, two_rows(q, even, odd), 0, 0) * 0.125
        gv = dot(pr.astype(BF16), gmx2, 0, 0)
        gq, gk, gv = gq.astype(BF16), gk.astype(BF16), gv.astype(BF16)
        out["gqkv"][:, cols] = gq
        out["gqkv"][:, kcols] = gk
        out["gqkv"][:, vcols] = gv
        gd[4:5, cols] = col_sum(gq.astype(F32))
        gd[5:6, cols] = col_sum(gv.astype(F32))

    wait_w(A)

    @matmul_loop(WIDTH, 256, 1)
    def _(cols):
        tmp["w"][:, cols] = dot(out["gqkv"][...], wa[:, cols], 1, 0)

    for i in range(4):
        r = slice(i * 32, (i + 1) * 32)
        ga1 = tmp["w"][r, :]
        gz, gg = norm_back(kept["zin"][r, :].astype(F32), pd[0:1, :], ga1)
        gd[0:1, :] += col_sum(gg)
        gd[3:4, :] += col_sum(ga1)
        out["gz"][r, :] = (gz + tmp["gz2"][r, :]).astype(BF16)
        send_out(i)

    ind = jnp.where(
        lax.broadcasted_iota(jnp.int32, (WIDTH, 128), 0) // 64 == lax.broadcasted_iota(jnp.int32, (WIDTH, 128), 1), 1.0, 0.0
    )
    hsum = lax.dot_general(
        jnp.broadcast_to(tmp["hs"][...], (8, WIDTH)), ind, (((1,), (0,)), ((), ())),
        precision=lax.Precision.HIGHEST, preferred_element_type=F32,
    )
    is13 = lax.broadcasted_iota(jnp.int32, (16, 128), 0) == 13
    out["gh"][...] = jnp.where(is13, jnp.concatenate([hsum, hsum], axis=0), 0.0)


KEEP = dict(
    zin=((TOK, WIDTH), BF16), a1=((TOK, WIDTH), BF16), qkv=((TOK, QKV), BF16), p=((8 * 256, TOK), F32),
    mixed=((TOK, WIDTH), F32), scaled=((TOK, WIDTH), BF16), attn=((TOK, WIDTH), F32), z2=((TOK, WIDTH), F32),
    a2=((TOK, WIDTH), BF16), hid=((TOK, FF), F32), mid=((TOK, FF), BF16), out=((TOK, WIDTH), BF16),
)
GRADS = dict(
    gin=((TOK, WIDTH), BF16), ghid=((TOK, FF), BF16), gattn=((TOK, WIDTH), BF16), gqkv=((TOK, QKV), BF16),
    gz=((TOK, WIDTH), BF16), gd=((16, WIDTH), F32), gm=((16, FF), F32), gh=((16, 128), F32),
)
WCLASS = (A, B, C, D)


def kernel_forward(*refs):
    own, refs = refs[:5], refs[5:]
    (tok, segc, segr, hs), refs = refs[:4], refs[4:]
    keep = dict(zip(KEEP, refs))
    refs = refs[len(KEEP) :]
    whbm, refs = refs[:4], refs[4:]
    (pd_out, pm_out), refs = refs[:2], refs[2:]
    bufs, refs = refs[:5], refs[5:]
    zin, send, recv, own_sem, xsend, xrecv, wsem = refs
    place = Place()
    loads = [
        pltpu.make_async_copy(own[k], part(bufs[k], ROWS[k], place.d, None), own_sem.at[k]) for k in range(5)
    ]
    for copy in loads:
        copy.start()
    place.barrier(True)
    for copy in loads:
        copy.wait()
    gather = Gather(place, bufs, send, recv)
    gather.run((S, A, B, C, D))
    for k in range(5):
        gather.whole(k)
    stores = [pltpu.make_async_copy(bufs[k], whbm[k - 1], wsem.at[k - 1]) for k in WCLASS]
    for copy in stores:
        copy.start()
    for q in range(8):
        at = slice(q * 128, (q + 1) * 128)
        acc = bufs[S][64 * q : 64 * q + 16, :]
        for j in range(1, 4):
            acc = acc + bufs[S][64 * q + 16 * j : 64 * q + 16 * j + 16, :]
        pd_out[:, at] = acc
    for q in range(32):
        pm_out[:, q * 128 : (q + 1) * 128] = bufs[S][16 * q : 16 * q + 16, :]

    def x_copy(n):
        cols = pl.ds(n * 256, 256)
        return remote(
            keep["out"].at[:, cols], zin.at[:, cols], xsend.at[n], xrecv.at[n], (place.s + 1) % 4, place.d
        )

    @pl.when(place.s == 0)
    def _():
        zin[...] = tok[...]

    @pl.when(place.s > 0)
    def _():
        for n in range(4):
            x_copy(n).wait_recv()

    keep["zin"][...] = zin[...]

    def send_out(n):
        @pl.when(place.s < 3)
        def _():
            x_copy(n).start()

    forward(zin, [bufs[k] for k in WCLASS], pd_out, pm_out, hs, segc, segr, keep, send_out)

    @pl.when(place.s < 3)
    def _():
        for n in range(4):
            x_copy(n).wait_send()

    gather.close()
    for copy in stores:
        copy.wait()


def kernel_backward(*refs):
    whbm, refs = refs[:4], refs[4:]
    kept = dict(zip(KEEP, refs))
    refs = refs[len(KEEP) :]
    (cot, pd, pm, hs), refs = refs[:4], refs[4:]
    out = dict(zip(GRADS, refs))
    refs = refs[len(GRADS) :]
    w, refs = refs[:4], refs[4:]
    gin, t_w, t_gz2, t_ff, t_hs, wsem, xsend, xrecv = refs
    place = Place()
    loads = {k: pltpu.make_async_copy(whbm[k - 1], w[k - 1], wsem.at[k - 1]) for k in (D, C, B, A)}
    for k in (D, C, B, A):
        loads[k].start()
    sem = pltpu.get_barrier_semaphore()
    for by in (1, 3):
        pl.semaphore_signal(sem, inc=1, device_id=((place.s + by) % 4, place.d), device_id_type=MESH)
    pl.semaphore_wait(sem, 2)

    def x_copy(i):
        r = pl.ds(i * 32, 32)
        return remote(out["gz"].at[r], gin.at[r], xsend.at[i], xrecv.at[i], (place.s + 3) % 4, place.d)

    @pl.when(place.s == 3)
    def _():
        gin[...] = cot[...]

    @pl.when(place.s < 3)
    def _():
        for i in range(4):
            x_copy(i).wait_recv()

    out["gin"][...] = gin[...]

    def send_out(i):
        @pl.when(place.s > 0)
        def _():
            x_copy(i).start()

    backward(
        gin, w, pd, pm, hs, kept, out, dict(w=t_w, gz2=t_gz2, ff=t_ff, hs=t_hs), lambda k: loads[k].wait(), send_out
    )

    @pl.when(place.s > 0)
    def _():
        for i in range(4):
            x_copy(i).wait_send()


class Scatter:
    def __init__(self, place, dw, sib, h1, f1, h2, f2, sem_send, sem_recv):
        self.p, self.dw, self.sib_buf = place, dw, sib
        self.h1, self.f1, self.h2, self.f2 = h1, f1, h2, f2
        self.send, self.recv = sem_send, sem_recv
        self.open = []


    def go(self, k, slot, src, dst, to):
        copy = remote(src, dst, self.send.at[k, slot], self.recv.at[k, slot], self.p.s, to)
        copy.start()
        self.open.append(copy)

    def got(self, k, slot, dst):
        remote(dst, dst, self.send.at[k, slot], self.recv.at[k, slot], self.p.s, self.p.sib).wait_recv()

    def block(self, k, of, og, half=None):
        return part(self.dw[k], ROWS[k], self.p.dp(of, og), half)

    def to_sibling(self, k):
        p = self.p
        for i in (3, 1, 2, 0):
            for j in (3, 1, 2, 0):
                slot = i * 4 + j
                src = part(self.dw[k], ROWS[k], p.sib_dp(OFFS[j], OFFS[i]), None)
                self.go(k, slot, src, part(self.sib_buf[k], ROWS[k], slot, None), p.sib)

    def add(self, k, dst, srcs, rows, store=None):
        cols = min(COLS[k], 1024)
        step = 16 if rows % 16 == 0 else 8
        steps_r, steps_c = rows // step, COLS[k] // cols

        def body(t, carry):
            r = pl.ds(pl.multiple_of((t // steps_c) * step, step), step)
            c = pl.ds(pl.multiple_of((t % steps_c) * cols, cols), cols)
            acc = dst[r, c].astype(F32)
            for src in srcs:
                acc = acc + src[r, c].astype(F32)
            if store is None:
                dst[r, c] = acc.astype(dst.dtype)
            else:
                store[r, c] = acc
            return carry

        lax.fori_loop(0, steps_r * steps_c, body, 0)

    def halves(self, k):
        p = self.p
        for j in (3, 1, 2, 0):
            slot = 3 * 4 + j
            here = part(self.sib_buf[k], ROWS[k], slot, None)
            self.got(k, slot, here)
            self.add(k, self.block(k, OFFS[j], 2), [here], ROWS[k])
            self.go(k, 16 + j, self.block(k, OFFS[j], 2, 0), part(self.h1[k], ROWS[k] // 2, j, None), p.dp(0, 1))
            self.go(k, 20 + j, self.block(k, OFFS[j], 2, 1), part(self.h1[k], ROWS[k] // 2, 4 + j, None), p.dp(0, 3))

    def wholes(self, k):
        p = self.p
        h = ROWS[k] // 2
        for j in (3, 1, 2, 0):
            for i, near, side in ((2, 1, 0), (1, 3, 1)):
                slot = i * 4 + j
                here = part(self.sib_buf[k], ROWS[k], slot, None)
                self.got(k, slot, here)
                hslot = 16 + 4 * side + j
                half = part(self.h1[k], h, 4 * side + j, None)
                self.got(k, hslot, half)
                blk = self.block(k, OFFS[j], near)
                self.add(k, blk.at[pl.ds(side * h, h)], [here.at[pl.ds(side * h, h)], half], h)
                self.add(k, blk.at[pl.ds((1 - side) * h, h)], [here.at[pl.ds((1 - side) * h, h)]], h)
                self.go(k, 24 + 4 * side + j, blk, part(self.f1[k], ROWS[k], 4 * side + j, None), p.dp(0, near))

    def settle(self, k, j):
        slot = j
        here = part(self.sib_buf[k], ROWS[k], slot, None)
        self.got(k, slot, here)
        srcs = [here]
        for side in range(2):
            src = part(self.f1[k], ROWS[k], 4 * side + j, None)
            self.got(k, 24 + 4 * side + j, src)
            srcs.append(src)
        self.add(k, self.block(k, OFFS[j], 0), srcs, ROWS[k])

    def far(self, k):
        p = self.p
        h = ROWS[k] // 2
        self.settle(k, 3)
        self.go(k, 32, self.block(k, 2, 0, 0), part(self.h2[k], h, 0, None), p.dp(1, 0))
        self.go(k, 33, self.block(k, 2, 0, 1), part(self.h2[k], h, 1, None), p.dp(3, 0))
        self.settle(k, 1)
        self.settle(k, 2)
        self.settle(k, 0)

    def near(self, k):
        p = self.p
        h = ROWS[k] // 2
        for near, side in ((1, 0), (3, 1)):
            half = part(self.h2[k], h, side, None)
            self.got(k, 32 + side, half)
            blk = self.block(k, near, 0)
            self.add(k, blk.at[pl.ds(side * h, h)], [half], h)
            self.go(k, 34 + side, blk, part(self.f2[k], ROWS[k], side, None), p.dp(near, 0))

    def last(self, k, out):
        srcs = []
        for side in range(2):
            src = part(self.f2[k], ROWS[k], side, None)
            self.got(k, 34 + side, src)
            srcs.append(src)
        self.add(k, self.block(k, 0, 0), srcs, ROWS[k], store=out)

    def close(self):
        for copy in self.open:
            copy.wait_send()


def kernel_grads(a1, scaled, a2, mid, gin, ghid, gattn, gqkv, gd, gm, gh, *refs):
    outs, refs = refs[:5], refs[5:]
    dw, refs = refs[:5], refs[5:]
    sib, refs = refs[:5], refs[5:]
    h1, refs = refs[:5], refs[5:]
    f1, refs = refs[:5], refs[5:]
    h2, refs = refs[:5], refs[5:]
    f2, refs = refs[:5], refs[5:]
    send, recv = refs
    place = Place()
    place.barrier(False)
    scatter = Scatter(place, dw, sib, h1, f1, h2, f2, send, recv)
    pairs = {A: (gqkv, a1), B: (gattn, scaled), C: (ghid, a2), D: (gin, mid)}

    def product(k):
        if k == S:

            @each(32)
            def _(d):
                at = pl.ds(pl.multiple_of((d // 4) * 128, 128), 128)
                own = pl.ds(pl.multiple_of(d * 128, 128), 128)
                dw[S][rows_of(d, 16), :] = gd[:, at] + gm[:, own] + gh[...]

            return
        g, a = pairs[k]
        rows, cols = 32 * ROWS[k], COLS[k]

        @each(rows // 512)
        def _(m):
            gt = g[:, pl.ds(pl.multiple_of(m * 512, 512), 512)].T

            @each(cols // 256)
            def _(n):
                at = pl.ds(pl.multiple_of(n * 256, 256), 256)
                dw[k][rows_of(m, 512), at] = dot(gt, a[:, at], 1, 0).astype(BF16)

    order = (D, C, B, A, S)
    n = len(order)
    for t in range(n + 4):
        if t < n:
            product(order[t])
            scatter.to_sibling(order[t])
        if 0 <= t - 1 < n:
            scatter.halves(order[t - 1])
        if 0 <= t - 2 < n:
            scatter.wholes(order[t - 2])
        if 0 <= t - 3 < n:
            scatter.far(order[t - 3])
            scatter.near(order[t - 3])
        if 0 <= t - 4 < n:
            scatter.last(order[t - 4], outs[order[t - 4]])
    scatter.close()


def vmem(shape, dtype):
    return pltpu.VMEM(shape, dtype)


VSPEC = pl.BlockSpec(memory_space=pltpu.VMEM)
ASPEC = pl.BlockSpec(memory_space=pl.ANY)
DMA = pltpu.SemaphoreType.DMA


def params(cid):
    return pltpu.CompilerParams(collective_id=cid, has_side_effects=True, vmem_limit_bytes=VMEM_LIMIT)


def struct(pair):
    return jax.ShapeDtypeStruct(*pair)


WSTRUCT = [((32 * ROWS[k], COLS[k]), BF16) for k in WCLASS]


def run_forward(own, tok, segc, segr, hs):
    outs = list(KEEP.values()) + WSTRUCT + [((16, WIDTH), F32), ((16, FF), F32)]
    return pl.pallas_call(
        kernel_forward,
        out_shape=[struct(o) for o in outs],
        in_specs=[ASPEC] * 5 + [VSPEC] * 4,
        out_specs=[VSPEC] * len(KEEP) + [ASPEC] * 4 + [VSPEC] * 2,
        scratch_shapes=[vmem((32 * ROWS[k], COLS[k]), TYPES[k]) for k in range(5)]
        + [vmem((TOK, WIDTH), BF16), DMA((5, 36)), DMA((5, 36)), DMA((5,)), DMA((4,)), DMA((4,)), DMA((4,))],
        compiler_params=params(1),
        name="gather_forward",
    )(*own, tok, segc, segr, hs)


def run_backward(weights, kept, cot, pd, pm, hs):
    return pl.pallas_call(
        kernel_backward,
        out_shape=[struct(o) for o in GRADS.values()],
        in_specs=[ASPEC] * 4 + [VSPEC] * (len(KEEP) + 4),
        out_specs=[VSPEC] * len(GRADS),
        scratch_shapes=[vmem(*w) for w in WSTRUCT]
        + [vmem((TOK, WIDTH), BF16), vmem((TOK, WIDTH), F32), vmem((TOK, WIDTH), F32), vmem((TOK, FF), F32)]
        + [vmem((1, WIDTH), F32), DMA((4,)), DMA((4,)), DMA((4,))],
        compiler_params=params(2),
        name="backward_chain",
    )(*weights, *kept, cot, pd, pm, hs)


def run_grads(*args):
    five = range(5)
    return pl.pallas_call(
        kernel_grads,
        out_shape=[jax.ShapeDtypeStruct((ROWS[k], COLS[k]), F32) for k in five],
        in_specs=[VSPEC] * 11,
        out_specs=[VSPEC] * 5,
        scratch_shapes=[vmem((32 * ROWS[k], COLS[k]), TYPES[k]) for k in five]
        + [vmem((16 * ROWS[k], COLS[k]), TYPES[k]) for k in five]
        + [vmem((8 * (ROWS[k] // 2), COLS[k]), TYPES[k]) for k in five]
        + [vmem((8 * ROWS[k], COLS[k]), TYPES[k]) for k in five]
        + [vmem((2 * (ROWS[k] // 2), COLS[k]), TYPES[k]) for k in five]
        + [vmem((2 * ROWS[k], COLS[k]), TYPES[k]) for k in five]
        + [DMA((5, 36)), DMA((5, 36))],
        compiler_params=params(3),
        name="grads_scatter",
    )(*args)


def body(
    tokens, cotangent, live_counts, segments, attn_input, attn_output, feed_up, feed_down,
    norm_gains, vector_bias, mid_gain, mid_bias, head_scale,
):
    d = lax.axis_index("dp")
    thin = jnp.concatenate([norm_gains[0], vector_bias[0]], axis=0).astype(F32)
    lane = d % 4
    spots = (jnp.arange(4) == lane).astype(F32)
    thin = (spots[None, :, None] * thin[:, None, :]).reshape(10, 128)
    small = jnp.concatenate(
        [thin, mid_gain[0][None].astype(F32), mid_bias[0].astype(F32), jnp.zeros((3, 128), F32)], axis=0
    )
    own = [small, attn_input[0].T, attn_output[0].T, feed_up[0].T, feed_down[0].T]
    hs = jnp.repeat(head_scale[0].astype(F32), 64)[None]
    live = jnp.repeat(live_counts, 64)
    place = jnp.arange(TOK) % 64
    cot = jnp.where((place < live)[:, None], cotangent, jnp.zeros_like(cotangent))
    fwd = run_forward(own, tokens, segments[:, None], segments[None, :], hs)
    kept = fwd[: len(KEEP)]
    weights = fwd[len(KEEP) : len(KEEP) + 4]
    pd, pm = fwd[len(KEEP) + 4 :]
    named = dict(zip(KEEP, kept))
    grads = run_backward(weights, kept, cot, pd, pm, hs)
    gn = dict(zip(GRADS, grads))
    sums = run_grads(
        named["a1"], named["scaled"], named["a2"], named["mid"], gn["gin"], gn["ghid"], gn["gattn"], gn["gqkv"],
        gn["gd"], gn["gm"], gn["gh"],
    )
    gs = lax.dynamic_slice(sums[S], (0, 32 * lane), (10, 32))
    return (
        named["out"][None],
        gn["gz"][None],
        sums[A].T[None],
        sums[B].T[None],
        sums[C].T[None],
        sums[D].T[None],
        gs[:3][None],
        gs[3:][None],
        sums[S][10:11],
        sums[S][11:13][None],
        sums[S][13:14, :16],
    )


def solution(mesh):
    return jax.shard_map(
        body,
        mesh=mesh,
        in_specs=(
            P("dp", None), P("dp", None), P("dp"), P("dp"),
            P("pipe", None, "dp"), P("pipe", None, "dp"), P("pipe", None, "dp"), P("pipe", None, "dp"),
            P("pipe", None, "dp"), P("pipe", None, "dp"), P("pipe", "dp"), P("pipe", None, "dp"), P("pipe", None),
        ),
        out_specs=(
            P("pipe", "dp", None), P("pipe", "dp", None),
            P("pipe", None, "dp"), P("pipe", None, "dp"), P("pipe", None, "dp"), P("pipe", None, "dp"),
            P("pipe", None, "dp"), P("pipe", None, "dp"), P("pipe", "dp"), P("pipe", None, "dp"), P("pipe", None),
        ),
        check_vma=False,
    )
```

time: 1430 us -> 407 us (0.28)
  waiting for transfers between devices: 747 us -> 0 us
  Pallas kernels: 0 us -> 380 us
  blocking collectives: 155 us -> 0 us
  matrix products: 154 us -> 0 us
  other arithmetic: 150 us -> 5.11 us
  local copies, waits for them, and re-layouts: 139 us -> 20 us
  starting transfers between devices: 45.8 us -> 0 us
  between operations: 16 us -> 0.71 us
    pallas_call x0 -> x3, Pallas kernels: none -> 380 us  [the longest x1 176 us: run_backward(): pl.pallas_call(kernel_backward, out_shape=[struct(o) for o in GRADS.value...]
    reduce_scatter x3 -> x0, waiting for transfers between devices: 263 us -> none  [the longest x1 94.3 us: body(): lax.psum_scatter(totals[3].astype(jnp.bfloat16), 'dp', scatter_dimension=...]
    ppermute x8 -> x0, waiting for transfers between devices: 223 us -> none  [passed_along(): return lax.ppermute(value, axis, pairs)]
    unnamed x15 -> x0, waiting for transfers between devices: 142 us -> none
    all_gather x4 -> x0, waiting for transfers between devices: 119 us -> none  [the longest x1 60.7 us: body(): lax.all_gather(feed_up[0], 'dp', axis=1, tiled=True)]
    dot_general x40 -> x0, matrix products: 118 us -> none  [the longest x4 22 us: layer_forward(): jnp.dot(normed_two, up_weight, preferred_element_type=jnp.float32)]
    convert_element_type x23 -> x5, other arithmetic: 107 us -> 2.68 us  [the longest x1 0.71 us: body(): thin = jnp.concatenate([norm_gains[0], vector_bias[0]], axis=0).astype(F32)]
    all_gather x4 -> x0, blocking collectives: 90 us -> none  [the longest x1 26.4 us: body(): lax.all_gather(norm_gains[0], 'dp', axis=1, tiled=True)]
  transfers between devices with their start and end apart: 19 -> 0, of which waited for: 16 -> 0; matrix products, arithmetic and copies ran while one was open for 9% -> 0% of each run, Pallas kernels for 0% -> 0%
where the time goes in v1:
time: 407 us; the launch traced here: 406 us
  Pallas kernels  380 us (93%)
  local copies, waits for them, and re-layouts  20 us (5%)
  other arithmetic  5.11 us (1%)
    pallas_call x1, Pallas kernels, run_backward(): pl.pallas_call(kernel_backward, out_shape=[struct(o) for o in GRADS.value...  176 us
    pallas_call x1, Pallas kernels, run_forward(): pl.pallas_call(kernel_forward, out_shape=[struct(o) for o in outs], in_sp...  108 us
    pallas_call x1, Pallas kernels, run_grads(): pl.pallas_call(kernel_grads, out_shape=[jax.ShapeDtypeStruct((ROWS[k], CO...  96.3 us
    unnamed x13, local copies, waits for them, and re-layouts  11.6 us

profile of v1, /device:TPU:0, one launch (start us, length us, event | category | flops | bytes accessed | tf_op | source)
XLA Modules:
  0.0 406.3 jit_solution(17551897505284803867)
XLA Ops:
  0.7 0.1 mul.20
  0.7 0.1 mul.21
  0.8 0.7 maximum_convert_fusion
  1.5 0.1 mul.24
  1.6 0.7 bitcast_convert_fusion.1
  2.3 0.1 pad.3.clone
  2.4 0.7 convert_element_type.31
  3.0 0.7 maximum_maximum_fusion.refs_0_
  3.7 0.7 bitcast_convert_fusion
  4.3 0.1 broadcast_in_dim.59
  4.4 0.7 broadcast_in_dim_reshape.3.refs_8_.refs_19_
  5.1 1.8 copy.24
  6.9 1.4 copy.25.refs_6_
  8.3 108.4 %gather_forward.1 = (bf16[128,1024]{1,0:T(8,128)(2,1)}, bf16[128,1024]{1,0:T(8,128)(2,1)}, bf16[128,3072]{1,0:T(8,128)(2,1)}, f32[2048,128]{1,0:T(8,128)}, f32[1...) custom-call(f32[16,128]{1,0:T(8,128)} %maximum_maximum_fusion.refs_0, ...), custom_call_target="tpu_custom_call" | custom-call | tf_op jit(solution)/shard_map/gather_forward/pallas_call | solution.py:723
  116.6 0.7 broadcast_in_dim.61
  117.4 0.1 reshape.68
  117.5 1.7 broadcast_select_fusion.refs_16_
  119.2 0.0 copy-start
  119.2 175.8 %backward_chain.1 = (bf16[128,1024]{1,0:T(8,128)(2,1)}, bf16[128,4096]{1,0:T(8,128)(2,1)}, bf16[128,1024]{1,0:T(8,128)(2,1)}, bf16[128,3072]{1,0:T(8,128)(2,1)},...) custom-call(bf16[3072,1024]{1,0:T(8,128)(2,1)} %get-tuple-element.43.refs_0_, ...), custom_call_target="tpu_custom_call" | custom-call | tf_op jit(solution)/shard_map/backward_chain/pallas_call | solution.py:736
  295.0 0.0 copy-start.1
  295.0 96.3 %grads_scatter.1 = (f32[16,128]{1,0:T(8,128)}, f32[96,1024]{1,0:T(8,128)}, f32[32,1024]{1,0:T(8,128)}, f32[128,1024]{1,0:T(8,128)}, f32[32,4096]{1,0:T(8,128)}) custom-call(bf16[128,1024]{1,0:T(8,128)(2,1)} %get-tuple-element.48.refs_5_.a1, bf16[128,1024]{1,0:T(8,128)(2,1)} %get-tuple-element.52.refs_9_.scaled, ...), custom_call_target="tpu_custom_call" | custom-call | tf_op jit(solution)/shard_map/grads_scatter/pallas_call | solution.py:751
  391.4 2.0 copy.26
  393.4 0.8 dynamic-slice_bitcast_fusion
  394.2 0.6 copy.28
  394.8 0.7 dynamic-slice_bitcast_fusion.1
  395.5 0.6 copy.27
  396.1 1.2 slice_bitcast_fusion
  397.3 1.2 slice.17
  398.5 1.2 slice.19
  399.7 0.0 copy-done
  399.7 0.7 copy.34
  400.4 0.0 copy-done.1
  400.4 0.7 copy.35
  401.1 1.8 copy.36
  402.9 1.6 copy.37
  404.4 1.9 copy.38
  (5 shorter events, 0.0 us)
Async XLA Ops:
  119.2 280.5 %copy-start = (bf16[128,1024]{1,0:T(8,128)(2,1)S(1)}, bf16[128,1024]{1,0:T(8,128)(2,1)}, u32[]{:S(2)}) copy-start(bf16[128,1024]{1,0:T(8,128)(2,1)} %get-tuple-element.42.refs_15_) | copy-start | bytes 786436
  295.0 105.4 %copy-start.1 = (bf16[128,1024]{1,0:T(8,128)(2,1)S(1)}, bf16[128,1024]{1,0:T(8,128)(2,1)}, u32[]{:S(2)}) copy-start(bf16[128,1024]{1,0:T(8,128)(2,1)} %get-tuple-element.60) | copy-start | bytes 786436

commit v2 on v1

v2 whole, which is shorter than its diff:
```python
import jax
import jax.numpy as jnp
from jax import lax
from jax.experimental import pallas as pl
from jax.experimental.pallas import tpu as pltpu
from jax.sharding import PartitionSpec as P

MESH = pl.DeviceIdType.MESH
EPS = 1e-05
F32, BF16 = jnp.float32, jnp.bfloat16
VMEM_LIMIT = 61800 * 1024

TOK, WIDTH, FF, QKV = 128, 1024, 4096, 3072
IN, OUT, UP, DOWN, UNITS = 0, 6, 8, 16, 24
SMALL = "small"
GATHER = (SMALL, (IN, 6), (OUT, 2), (UP, 8), (DOWN, 8))
SCATTER = ((DOWN, 4), (DOWN + 4, 4), (UP, 4), (UP + 4, 4), (IN, 4), (IN + 4, 4), SMALL)
SHARE = 3
OFFS = (0, 3, 1, 2)


class Place:
    def __init__(self):
        self.s = lax.axis_index("pipe")
        d = lax.axis_index("dp")
        self.d = d
        self.c = d % 2
        y, z = (d // 2) % 4, d // 8
        self.f = y + self.c * (z - y)
        self.g = z + self.c * (y - z)
        self.sf = 2 + 6 * self.c
        self.sg = 8 - 6 * self.c
        self.sib = d + 1 - 2 * self.c

    def dp(self, of, og):
        return ((self.f + of) % 4) * self.sf + ((self.g + og) % 4) * self.sg + self.c

    def sib_dp(self, of, og):
        return ((self.g + of) % 4) * self.sg + ((self.f + og) % 4) * self.sf + 1 - self.c

    def barrier(self):
        sem = pltpu.get_barrier_semaphore()
        near = [self.dp(1, 0), self.dp(3, 0), self.dp(0, 1), self.dp(0, 3), self.sib]
        near = [(self.s, to) for to in near] + [((self.s + by) % 4, self.d) for by in (1, 3)]
        for to in near:
            pl.semaphore_signal(sem, inc=1, device_id=to, device_id_type=MESH)
        pl.semaphore_wait(sem, len(near))


def remote(src, dst, send, recv, s, to):
    return pltpu.make_async_remote_copy(
        src_ref=src, dst_ref=dst, send_sem=send, recv_sem=recv, device_id=(s, to), device_id_type=MESH
    )


def piece_block(whole, small, piece, d, half=None):
    if piece is SMALL:
        return small.at[d] if half is None else small.at[d, pl.ds(8 * half, 8)]
    u, n = piece
    return whole.at[d, pl.ds(u, n)] if half is None else whole.at[d, pl.ds(u + half * (n // 2), n // 2)]


class Gather:
    def __init__(self, place, whole, small, send, recv):
        self.p, self.whole_ref, self.small = place, whole, small
        self.send, self.recv = send, recv
        self.open = []

    def ref(self, k, d, half):
        return piece_block(self.whole_ref, self.small, GATHER[k], d, half)

    def put(self, k, slot, d, half, to):
        ref = self.ref(k, d, half)
        copy = remote(ref, ref, self.send.at[k, slot], self.recv.at[k, slot], self.p.s, to)
        copy.start()
        self.open.append(copy)

    def got(self, k, slot, d, half):
        ref = self.ref(k, d, half)
        remote(ref, ref, self.send.at[k, slot], self.recv.at[k, slot], self.p.s, self.p.sib).wait_recv()

    def spread(self, k, j):
        p = self.p
        d = p.dp(OFFS[j], 0)
        self.put(k, 4 + 4 * j, d, None, p.dp(0, 1))
        self.put(k, 5 + 4 * j, d, None, p.dp(0, 3))
        self.put(k, 20 + 4 * j, d, None, p.sib)

    def first(self, k):
        p = self.p
        self.put(k, 0, p.d, None, p.dp(1, 0))
        self.put(k, 1, p.d, None, p.dp(3, 0))
        self.spread(k, 0)

    def ring(self, k):
        p = self.p
        left, right = p.dp(3, 0), p.dp(1, 0)
        self.got(k, 0, left, None)
        self.put(k, 2, left, 0, right)
        self.spread(k, 1)
        self.got(k, 1, right, None)
        self.put(k, 3, right, 1, left)
        self.spread(k, 2)

    def far(self, k):
        d = self.p.dp(2, 0)
        self.got(k, 2, d, 0)
        self.got(k, 3, d, 1)
        self.spread(k, 3)

    def second(self, k):
        p = self.p
        for j in range(4):
            low, high = p.dp(OFFS[j], 3), p.dp(OFFS[j], 1)
            self.got(k, 4 + 4 * j, low, None)
            self.put(k, 6 + 4 * j, low, 0, p.dp(0, 1))
            self.put(k, 21 + 4 * j, low, None, p.sib)
            self.got(k, 5 + 4 * j, high, None)
            self.put(k, 7 + 4 * j, high, 1, p.dp(0, 3))
            self.put(k, 22 + 4 * j, high, None, p.sib)

    def last(self, k):
        p = self.p
        for j in range(4):
            d = p.dp(OFFS[j], 2)
            self.got(k, 6 + 4 * j, d, 0)
            self.got(k, 7 + 4 * j, d, 1)
            self.put(k, 23 + 4 * j, d, None, p.sib)

    def whole(self, k):
        for j in range(4):
            for i in range(4):
                self.got(k, 20 + 4 * j + i, self.p.sib_dp(OFFS[j], OFFS[i]), None)

    def close(self):
        for copy in self.open:
            copy.wait_send()

    def run(self, ready):
        n, begun = len(GATHER), 0
        for t in range(n + 3):
            while begun < min(n, t + 3):
                self.first(begun)
                begun += 1
            if t < n:
                self.ring(t)
            if 0 <= t - 1 < n:
                self.far(t - 1)
            if 0 <= t - 2 < n:
                self.second(t - 2)
            if 0 <= t - 3 < n:
                self.last(t - 3)
                self.whole(t - 3)
                ready(t - 3)


def dot(a, b, ca, cb):
    return lax.dot_general(a, b, (((ca,), (cb,)), ((), ())), preferred_element_type=F32)


def centered(x):
    c = x - jnp.mean(x, axis=-1, keepdims=True)
    r = lax.rsqrt(jnp.mean(c * c, axis=-1, keepdims=True) + EPS)
    return c, r


def norm(x, gain, bias):
    c, r = centered(x)
    return c * r * gain + bias


def norm_back(x, gain, gy):
    c, r = centered(x)
    hat = c * r
    gh = gy * gain
    gx = r * (gh - jnp.mean(gh, axis=-1, keepdims=True) - hat * jnp.mean(gh * hat, axis=-1, keepdims=True))
    return gx, gy * hat


def rows_of(i, n):
    return pl.ds(pl.multiple_of(i * n, n), n)


def col_sum(x):
    return jnp.sum(x, axis=0, keepdims=True)


def row_sum(x):
    return dot(jnp.full((16, x.shape[0]), 1.0, BF16), x, 1, 0)[:1]


K0, K1 = 0.7978845608028654, 0.044715


def gelu(x):
    return 0.5 * x * (1.0 + jnp.tanh(K0 * (x + K1 * x * x * x)))


def gelu_both(x):
    t = jnp.tanh(K0 * (x + K1 * x * x * x))
    u = 0.5 * x * (1.0 + t)
    du = 0.5 * (1.0 + t) + 0.5 * x * (1.0 - t * t) * K0 * (1.0 + 3.0 * K1 * x * x)
    return u, du


def head_masks():
    lane = lax.broadcasted_iota(jnp.int32, (1, 128), 1)
    even = jnp.where(lane < 64, 1.0, 0.0)
    return even.astype(BF16), (1.0 - even).astype(BF16)


def two_rows(x, even, odd):
    return jnp.concatenate([x * even, x * odd], axis=0)


def each(count, unroll=1):
    def run(body):
        def step(i, carry):
            body(i)
            return carry

        lax.fori_loop(0, count, step, 0, unroll=unroll)

    return run


def stack(w, d0, nd, u, nu):
    return w[pl.ds(d0, nd), u : u + nu].reshape(nd * nu * 16, WIDTH)


def head_columns():
    col = lax.broadcasted_iota(jnp.int32, (128, WIDTH), 1)
    head = lax.broadcasted_iota(jnp.int32, (128, WIDTH), 0)
    return jnp.where(col // 64 == head, 1.0, 0.0)


class Layer:
    def __init__(self, w, r):
        self.w, self.r = w, r


    def first_norm(self):
        r, pd = self.r, self.r["pd"]

        @each(4, 2)
        def _(i):
            at = rows_of(i, 32)
            r["a1"][at, :] = norm(r["zin"][at, :].astype(F32), pd[0:1, :], pd[3:4, :]).astype(BF16)

    def qkv(self):
        r = self.r
        for c in range(4):
            at = slice(c * 768, (c + 1) * 768)
            acc = dot(r["a1"][...], stack(self.w, 8 * c, 8, IN, 6), 1, 1) + r["pq"][0:1, at]
            r["qkv"][:, at] = acc.astype(BF16)

    def attention(self):
        r, qkv = self.r, self.r["qkv"]
        even, odd = head_masks()

        @each(8, 4)
        def _(p):
            cols = rows_of(p, 128)
            q = qkv[:, cols]
            k = qkv[:, pl.ds(pl.multiple_of(WIDTH + p * 128, 128), 128)]
            v = qkv[:, pl.ds(pl.multiple_of(2 * WIDTH + p * 128, 128), 128)]
            ok = r["ok"][...]
            sc = dot(two_rows(q, even, odd), k, 1, 1) * 0.125
            sc = jnp.where(jnp.concatenate([ok, ok], axis=0) > 0.5, sc, -1000000000.0)
            e = jnp.exp(sc - jnp.max(sc, axis=-1, keepdims=True))
            pr = e / jnp.sum(e, axis=-1, keepdims=True)
            r["p"][rows_of(p, 256), :] = pr
            pb = pr.astype(BF16)
            both = jnp.concatenate([pb[:TOK], pb[TOK:]], axis=1)
            mixed = dot(both, two_rows(v, even, odd), 1, 0)
            r["mixed"][:, cols] = mixed
            r["scaled"][:, cols] = (mixed * r["hs"][0:1, cols]).astype(BF16)

    def project(self):
        r = self.r
        r["attn"][...] = dot(r["scaled"][...], stack(self.w, 0, 32, OUT, 2), 1, 1) + r["pd"][6:7, :]

    def middle_norms(self):
        r, pd = self.r, self.r["pd"]

        @each(4, 2)
        def _(i):
            at = rows_of(i, 32)
            z2 = r["zin"][at, :].astype(F32) + norm(r["attn"][at, :], pd[1:2, :], pd[7:8, :])
            r["z2"][at, :] = z2
            r["a2"][at, :] = norm(z2, pd[2:3, :], pd[8:9, :]).astype(BF16)

    def up(self):
        r = self.r

        @each(4)
        def _(c):
            cols = rows_of(c, 1024)
            r["ff"][:, cols] = dot(r["a2"][...], stack(self.w, 8 * c, 8, UP, 8), 1, 1) + r["pm"][11:12, cols]

    def inner_norm(self):
        r, pm = self.r, self.r["pm"]

        @each(8, 2)
        def _(i):
            at = rows_of(i, 16)
            r["mid"][at, :] = norm(gelu(r["ff"][at, :]), pm[10:11, :], pm[12:13, :]).astype(BF16)

    def down(self, send_out):
        r = self.r
        for n in range(4):
            cols = slice(n * 256, (n + 1) * 256)
            acc = r["z2"][:, cols] + r["pd"][9:10, cols]
            for q in range(4):
                w = stack(self.w, 8 * n, 8, DOWN + 2 * q, 2)
                acc = acc + dot(r["mid"][:, q * 1024 : (q + 1) * 1024], w, 1, 1)
            r["out"][:, cols] = acc.astype(BF16)
            send_out(n)

    def prepare(self):
        r = self.r

        @each(8, 2)
        def _(i):
            at = rows_of(i, 16)
            u, du = gelu_both(r["ff"][at, :])
            c, s = centered(u)
            r["hat"][at, :] = (c * s).astype(BF16)
            r["slope"][at, :] = (du * s).astype(BF16)

        for name in ("gd", "gm"):
            r[name][...] = jnp.zeros_like(r[name])


    def back_down(self):
        r = self.r
        for q in range(4):
            w = stack(self.w, 0, 32, DOWN + 2 * q, 2)
            r["ff"][:, q * 1024 : (q + 1) * 1024] = dot(r["gin"][...], w, 1, 0)

    def back_inner(self):
        r, pm = self.r, self.r["pm"]

        @each(8, 2)
        def _(i):
            at = rows_of(i, 16)
            gh = r["ff"][at, :] * pm[10:11, :]
            hat = r["hat"][at, :].astype(F32)
            m1 = jnp.mean(gh, axis=-1, keepdims=True)
            m2 = jnp.mean(gh * hat, axis=-1, keepdims=True)
            r["ghid"][at, :] = ((gh - m1 - hat * m2) * r["slope"][at, :].astype(F32)).astype(BF16)

    def back_up(self):
        r = self.r
        r["tw"][...] = dot(r["ghid"][...], stack(self.w, 0, 32, UP, 8), 1, 0)

    def back_middle(self):
        r, gd, pd = self.r, self.r["gd"], self.r["pd"]

        @each(4, 2)
        def _(i):
            at = rows_of(i, 32)
            ga2 = r["tw"][at, :]
            gz, gg = norm_back(r["z2"][at, :], pd[2:3, :], ga2)
            gd[2:3, :] += col_sum(gg)
            gd[8:9, :] += col_sum(ga2)
            gz = gz + r["gin"][at, :].astype(F32)
            r["gz2"][at, :] = gz
            gat, gg = norm_back(r["attn"][at, :], pd[1:2, :], gz)
            gd[1:2, :] += col_sum(gg)
            gd[7:8, :] += col_sum(gz)
            r["gattn"][at, :] = gat.astype(BF16)

    def back_project(self):
        r = self.r
        r["tw"][...] = dot(r["gattn"][...], stack(self.w, 0, 32, OUT, 2), 1, 0)

    def back_attention(self):
        r = self.r
        even, odd = head_masks()

        @each(8, 4)
        def _(p):
            cols = rows_of(p, 128)
            kcols = pl.ds(pl.multiple_of(WIDTH + p * 128, 128), 128)
            vcols = pl.ds(pl.multiple_of(2 * WIDTH + p * 128, 128), 128)
            gs = r["tw"][:, cols]
            r["gh"][0:1, cols] = col_sum(gs * r["mixed"][:, cols])
            gmx = (gs * r["hs"][0:1, cols]).astype(BF16)
            q, k, v = r["qkv"][:, cols], r["qkv"][:, kcols], r["qkv"][:, vcols]
            gmx2 = two_rows(gmx, even, odd)
            gp = dot(gmx2, v, 1, 1)
            pr = r["p"][rows_of(p, 256), :]
            gsc = (pr * (gp - jnp.sum(pr * gp, axis=-1, keepdims=True))).astype(BF16)
            both = jnp.concatenate([gsc[:TOK], gsc[TOK:]], axis=1)
            r["gqkv"][:, cols] = (dot(both, two_rows(k, even, odd), 1, 0) * 0.125).astype(BF16)
            r["gqkv"][:, kcols] = (dot(gsc, two_rows(q, even, odd), 0, 0) * 0.125).astype(BF16)
            r["gqkv"][:, vcols] = dot(pr.astype(BF16), gmx2, 0, 0).astype(BF16)

    def back_qkv(self):
        r = self.r
        r["tw"][...] = dot(r["gqkv"][...], stack(self.w, 0, 32, IN, 6), 1, 0)

    def back_first(self, send_out):
        r, gd, pd = self.r, self.r["gd"], self.r["pd"]
        for i in range(4):
            at = slice(i * 32, (i + 1) * 32)
            ga1 = r["tw"][at, :]
            gz, gg = norm_back(r["zin"][at, :].astype(F32), pd[0:1, :], ga1)
            r["gz"][at, :] = (gz + r["gz2"][at, :]).astype(BF16)
            send_out(i)
            gd[0:1, :] += col_sum(gg)
            gd[3:4, :] += col_sum(ga1)

    def inner_sums(self):
        r, gm = self.r, self.r["gm"]

        @each(8)
        def _(i):
            at = rows_of(i, 16)
            g = r["ff"][at, :]
            gm[10:11, :] += col_sum(g * r["hat"][at, :].astype(F32))
            gm[12:13, :] += col_sum(g)

        gm[11:12, :] = row_sum(r["ghid"][...])

    def other_sums(self):
        r, gd = self.r, self.r["gd"]
        gd[9:10, :] = row_sum(r["gin"][...])
        gd[6:7, :] = row_sum(r["gattn"][...])
        gd[4:5, :] = row_sum(r["gqkv"][:, :WIDTH])
        gd[5:6, :] = row_sum(r["gqkv"][:, 2 * WIDTH :])


    def grad_down(self):
        r = self.r

        @each(4)
        def _(c):
            gt = r["gin"][:, rows_of(c, 256)].T
            for q in range(4):
                g = dot(gt, r["mid"][:, q * 1024 : (q + 1) * 1024], 1, 0).astype(BF16)
                self.w[pl.ds(8 * c, 8), DOWN + 2 * q : DOWN + 2 * q + 2] = g.reshape(8, 2, 16, WIDTH)

    def grad_up(self):
        r = self.r

        @each(8)
        def _(c):
            gt = r["ghid"][:, rows_of(c, 512)].T
            g = dot(gt, r["a2"][...], 1, 0).astype(BF16)
            self.w[pl.ds(4 * c, 4), UP : UP + 8] = g.reshape(4, 8, 16, WIDTH)

    def grad_attention(self):
        r = self.r

        @each(8)
        def _(c):
            gt = r["gqkv"][:, rows_of(c, 384)].T
            g = dot(gt, r["a1"][...], 1, 0).astype(BF16)
            self.w[pl.ds(4 * c, 4), IN : IN + 6] = g.reshape(4, 6, 16, WIDTH)

        @each(2)
        def _(c):
            gt = r["gattn"][:, rows_of(c, 512)].T
            g = dot(gt, r["scaled"][...], 1, 0).astype(BF16)
            self.w[pl.ds(16 * c, 16), OUT : OUT + 2] = g.reshape(16, 2, 16, WIDTH)

    def grad_small(self, small):
        r = self.r
        hsum = lax.dot_general(
            jnp.broadcast_to(r["gh"][0:1, :], (8, WIDTH)), head_columns(), (((1,), (1,)), ((), ())),
            precision=lax.Precision.HIGHEST, preferred_element_type=F32,
        )
        is13 = lax.broadcasted_iota(jnp.int32, (16, 128), 0) == 13
        heads = jnp.where(is13, jnp.concatenate([hsum, hsum], axis=0), 0.0)
        for d in range(32):
            a, b = (d // 4) * 128, d * 128
            small[d] = r["gd"][:, a : a + 128] + r["gm"][:, b : b + 128] + heads


class Scatter:
    def __init__(self, place, grads, small, sib, ssib, land, sland, send, recv):
        self.p, self.grads, self.small = place, grads, small
        self.sib, self.ssib, self.land, self.sland = sib, ssib, land, sland
        self.send, self.recv = send, recv
        self.open = []

    def go(self, k, slot, src, dst, to):
        copy = remote(src, dst, self.send.at[k, slot], self.recv.at[k, slot], self.p.s, to)
        copy.start()
        self.open.append(copy)

    def got(self, k, slot, dst):
        remote(dst, dst, self.send.at[k, slot], self.recv.at[k, slot], self.p.s, self.p.sib).wait_recv()

    def block(self, k, of, og, half=None):
        return piece_block(self.grads, self.small, SCATTER[k], self.p.dp(of, og), half)

    def from_sib(self, k, slot, half=None):
        return piece_block(self.sib, self.ssib, SCATTER[k], slot, half)

    def landing(self, k, kind, slot):
        if SCATTER[k] is SMALL:
            ref = self.sland[kind].at[slot]
        else:
            ref = self.land[kind].at[k % SHARE, slot]
        return ref

    def to_sibling(self, k):
        p = self.p
        for i in (3, 1, 2, 0):
            for j in (3, 1, 2, 0):
                src = piece_block(self.grads, self.small, SCATTER[k], p.sib_dp(OFFS[j], OFFS[i]))
                self.go(k, i * 4 + j, src, self.from_sib(k, i * 4 + j), p.sib)

    def add(self, k, dst, srcs, store=None):
        out = dst if store is None else store
        if SCATTER[k] is SMALL:
            out[...] = dst[...] + sum(src[...] for src in srcs)
            return
        for u in range(dst.shape[0]):
            acc = dst[u].astype(F32)
            for src in srcs:
                acc = acc + src[u].astype(F32)
            out[u] = acc.astype(out.dtype)

    def halves(self, k):
        p = self.p
        for j in (3, 1, 2, 0):
            slot = 3 * 4 + j
            here = self.from_sib(k, slot)
            self.got(k, slot, here)
            self.add(k, self.block(k, OFFS[j], 2), [here])
            self.go(k, 16 + j, self.block(k, OFFS[j], 2, 0), self.landing(k, 0, j), p.dp(0, 1))
            self.go(k, 20 + j, self.block(k, OFFS[j], 2, 1), self.landing(k, 0, 4 + j), p.dp(0, 3))

    def wholes(self, k):
        p = self.p
        for j in (3, 1, 2, 0):
            for i, side in ((2, 0), (1, 1)):
                self.got(k, i * 4 + j, self.from_sib(k, i * 4 + j))
                self.got(k, 16 + 4 * side + j, self.landing(k, 0, 4 * side + j))
            for i, near, side in ((2, 1, 0), (1, 3, 1)):
                slot = i * 4 + j
                self.add(
                    k, self.block(k, OFFS[j], near, side), [self.from_sib(k, slot, side), self.landing(k, 0, 4 * side + j)]
                )
                self.add(k, self.block(k, OFFS[j], near, 1 - side), [self.from_sib(k, slot, 1 - side)])
            for near, side in ((1, 0), (3, 1)):
                self.go(
                    k, 24 + 4 * side + j, self.block(k, OFFS[j], near), self.landing(k, 1, 4 * side + j), p.dp(0, near)
                )

    def settle(self, k, j):
        here = self.from_sib(k, j)
        self.got(k, j, here)
        srcs = [here]
        for side in range(2):
            src = self.landing(k, 1, 4 * side + j)
            self.got(k, 24 + 4 * side + j, src)
            srcs.append(src)
        self.add(k, self.block(k, OFFS[j], 0), srcs)

    def far(self, k):
        p = self.p
        self.settle(k, 3)
        self.go(k, 32, self.block(k, 2, 0, 0), self.landing(k, 2, 0), p.dp(1, 0))
        self.go(k, 33, self.block(k, 2, 0, 1), self.landing(k, 2, 1), p.dp(3, 0))
        for j in (1, 2, 0):
            self.settle(k, j)

    def near(self, k):
        p = self.p
        for side in range(2):
            self.got(k, 32 + side, self.landing(k, 2, side))
        for near, side in ((1, 0), (3, 1)):
            self.add(k, self.block(k, near, 0, side), [self.landing(k, 2, side)])
        for near, side in ((1, 0), (3, 1)):
            self.go(k, 34 + side, self.block(k, near, 0), self.landing(k, 3, side), p.dp(near, 0))

    def last(self, k, total, small_total):
        srcs = []
        for side in range(2):
            src = self.landing(k, 3, side)
            self.got(k, 34 + side, src)
            srcs.append(src)
        if SCATTER[k] is SMALL:
            store = small_total
        else:
            u, n = SCATTER[k]
            store = total.at[pl.ds(u, n)]
        self.add(k, self.block(k, 0, 0), srcs, store=store)

    def close(self):
        for copy in self.open:
            copy.wait_send()


HELD = dict(
    pd=((16, WIDTH), F32), pm=((16, FF), F32), pq=((1, QKV), F32), hs=((8, WIDTH), F32), ok=((TOK, TOK), F32),
    zin=((TOK, WIDTH), BF16), a1=((TOK, WIDTH), BF16), qkv=((TOK, QKV), BF16), p=((8 * 256, TOK), F32),
    mixed=((TOK, WIDTH), F32), scaled=((TOK, WIDTH), BF16), attn=((TOK, WIDTH), F32), z2=((TOK, WIDTH), F32),
    a2=((TOK, WIDTH), BF16), ff=((TOK, FF), F32), hat=((TOK, FF), BF16), slope=((TOK, FF), BF16), mid=((TOK, FF), BF16),
    gin=((TOK, WIDTH), BF16), ghid=((TOK, FF), BF16), gattn=((TOK, WIDTH), BF16), gqkv=((TOK, QKV), BF16),
    tw=((TOK, WIDTH), F32), gz2=((TOK, WIDTH), F32), gd=((16, WIDTH), F32), gm=((16, FF), F32), gh=((8, WIDTH), F32),
)
LANDING = ((8, 2), (8, 4), (2, 2), (2, 4))


def kernel(*refs):
    (tok, cot, live, seg, own_in, own_out, own_up, own_down, gains, vecs, mgain, mbias, hscale), refs = refs[:13], refs[13:]
    (out, gz, total, small_total), refs = refs[:4], refs[4:]
    (w, small, sib, ssib), refs = refs[:4], refs[4:]
    land, sland, refs = refs[:4], refs[4:8], refs[8:]
    r = dict(zip(HELD, refs), out=out, gz=gz)
    gsend, grecv, own_sem, xsend, xrecv, bsend, brecv, ssend, srecv = refs[len(HELD) :]
    place = Place()
    layer = Layer(w, r)

    loads = [
        pltpu.make_async_copy(own_in, w.at[place.d, pl.ds(IN, 6)], own_sem.at[0]),
        pltpu.make_async_copy(own_out, w.at[place.d, pl.ds(OUT, 2)], own_sem.at[1]),
    ] + [
        pltpu.make_async_copy(
            own_down.at[:, :, pl.ds(q * 1024, 1024)], w.at[place.d, pl.ds(DOWN + 2 * q, 2)], own_sem.at[2 + q]
        )
        for q in range(4)
    ]
    for copy in loads:
        copy.start()
    token_load = pltpu.make_async_copy(tok, r["zin"], own_sem.at[6])
    cot_load = pltpu.make_async_copy(cot, r["gin"], own_sem.at[7])

    @pl.when(place.s == 0)
    def _():
        token_load.start()

    @pl.when(place.s == 3)
    def _():
        cot_load.start()

    w[place.d, UP : UP + 8] = own_up[...].T.reshape(8, 16, WIDTH)
    mine = lax.broadcasted_iota(jnp.int32, (1, 128), 1) // 32 == place.d % 4

    def spot(x):
        x = x.astype(F32)
        return jnp.where(mine, jnp.concatenate([x, x, x, x], axis=1), 0.0)

    small[place.d, 0:3] = spot(gains[...])
    small[place.d, 3:10] = spot(vecs[...])
    small[place.d, 10:11] = mgain[...].astype(F32)
    small[place.d, 11:13] = mbias[...].astype(F32)
    small[place.d, 13:16] = jnp.zeros((3, 128), F32)
    place.barrier()
    for copy in loads:
        copy.wait()

    def forward_copy(n):
        cols = pl.ds(n * 256, 256)
        return remote(
            out.at[:, cols], r["zin"].at[:, cols], xsend.at[n], xrecv.at[n], (place.s + 1) % 4, place.d
        )

    def send_forward(n):
        @pl.when(place.s < 3)
        def _():
            forward_copy(n).start()

    gather = Gather(place, w, small, gsend, grecv)

    def setup():
        for q in range(8):
            r["pd"][:, q * 128 : (q + 1) * 128] = small[4 * q] + small[4 * q + 1] + small[4 * q + 2] + small[4 * q + 3]
        for q in range(32):
            r["pm"][:, q * 128 : (q + 1) * 128] = small[q]
        r["pq"][:, :WIDTH] = r["pd"][4:5, :]
        r["pq"][:, WIDTH : 2 * WIDTH] = jnp.zeros((1, WIDTH), F32)
        r["pq"][:, 2 * WIDTH :] = r["pd"][5:6, :]
        heads = jnp.concatenate([hscale[...].astype(F32), jnp.zeros((1, 112), F32)], axis=1)
        r["hs"][...] = lax.dot_general(
            jnp.broadcast_to(heads, (8, 128)), head_columns(), (((1,), (0,)), ((), ())),
            precision=lax.Precision.HIGHEST, preferred_element_type=F32,
        )
        row = lax.broadcasted_iota(jnp.int32, (TOK, TOK), 0)
        col = lax.broadcasted_iota(jnp.int32, (TOK, TOK), 1)
        seg_key = jnp.broadcast_to(seg[...].astype(F32), (TOK, TOK))
        ok = (seg_key == seg_key.T) & (col <= row) & (row // 64 == col // 64)
        r["ok"][...] = jnp.where(ok, 1.0, 0.0)

    def ready(k):
        if k == 0:
            setup()

        @pl.when(place.s == 0)
        def _():
            if k == 0:
                token_load.wait()
                layer.first_norm()
            elif k == 1:
                layer.qkv()
                layer.attention()
            elif k == 2:
                layer.project()
                layer.middle_norms()
            elif k == 3:
                layer.up()
                layer.inner_norm()
            else:
                layer.down(send_forward)

    gather.run(ready)

    @pl.when(place.s > 0)
    def _():
        for n in range(4):
            forward_copy(n).wait_recv()
        layer.first_norm()
        layer.qkv()
        layer.attention()
        layer.project()
        layer.middle_norms()
        layer.up()
        layer.inner_norm()
        layer.down(send_forward)

    layer.prepare()
    gather.close()

    @pl.when(place.s < 3)
    def _():
        for n in range(4):
            forward_copy(n).wait_send()

    def backward_copy(i):
        at = pl.ds(i * 32, 32)
        return remote(gz.at[at], r["gin"].at[at], bsend.at[i], brecv.at[i], (place.s + 3) % 4, place.d)

    def send_backward(i):
        @pl.when(place.s > 0)
        def _():
            backward_copy(i).start()

    @pl.when(place.s == 3)
    def _():
        cot_load.wait()

        @each(4)
        def _(i):
            at = rows_of(i, 32)
            row = lax.broadcasted_iota(jnp.int32, (32, WIDTH), 0) + 32 * i
            alive = row % 64 < jnp.where(row < 64, live[0], live[1])
            r["gin"][at, :] = jnp.where(alive, r["gin"][at, :].astype(F32), 0.0).astype(BF16)

    @pl.when(place.s < 3)
    def _():
        for i in range(4):
            backward_copy(i).wait_recv()

    @pl.when(place.s > 0)
    def _():
        layer.back_down()
        layer.back_inner()
        layer.back_up()
        layer.back_middle()
        layer.back_project()
        layer.back_attention()
        layer.back_qkv()
        layer.back_first(send_backward)

    def first_section(*phases):
        @pl.when(place.s == 0)
        def _():
            for phase in phases:
                phase()

    scatter = Scatter(place, w, small, sib, ssib, land, sland, ssend, srecv)
    n = len(SCATTER)

    def flow(t):
        if 0 <= t - 1 < n:
            scatter.halves(t - 1)
        if 0 <= t - 2 < n:
            scatter.wholes(t - 2)
        if 0 <= t - 3 < n:
            scatter.far(t - 3)
        if 0 <= t - 4 < n:
            scatter.near(t - 4)
        if 0 <= t - 5 < n:
            scatter.last(t - 5, total, small_total)

    first_section(layer.back_down)
    layer.grad_down()
    scatter.to_sibling(0)
    scatter.to_sibling(1)
    first_section(layer.back_inner, layer.back_up)
    flow(1)
    layer.grad_up()
    scatter.to_sibling(2)
    scatter.to_sibling(3)
    flow(2)
    first_section(layer.back_middle, layer.back_project)
    flow(3)
    first_section(layer.back_attention)
    flow(4)
    first_section(layer.back_qkv, lambda: layer.back_first(send_backward))
    layer.grad_attention()
    scatter.to_sibling(4)
    scatter.to_sibling(5)
    flow(5)
    layer.inner_sums()
    layer.other_sums()
    layer.grad_small(small)
    scatter.to_sibling(6)
    for t in range(6, n + 5):
        flow(t)
    scatter.close()

    @pl.when(place.s > 0)
    def _():
        for i in range(4):
            backward_copy(i).wait_send()


VSPEC = pl.BlockSpec(memory_space=pltpu.VMEM)
ASPEC = pl.BlockSpec(memory_space=pl.ANY)
SSPEC = pl.BlockSpec(memory_space=pltpu.SMEM)
DMA = pltpu.SemaphoreType.DMA


def run_layers(*args):
    g, s = (len(GATHER), 36), (len(SCATTER), 36)
    return pl.pallas_call(
        kernel,
        out_shape=[
            jax.ShapeDtypeStruct((TOK, WIDTH), BF16),
            jax.ShapeDtypeStruct((TOK, WIDTH), BF16),
            jax.ShapeDtypeStruct((UNITS, 16, WIDTH), F32),
            jax.ShapeDtypeStruct((16, 128), F32),
        ],
        in_specs=[ASPEC, ASPEC, SSPEC, VSPEC, ASPEC, ASPEC, VSPEC, ASPEC, VSPEC, VSPEC, VSPEC, VSPEC, VSPEC],
        out_specs=[VSPEC] * 4,
        scratch_shapes=[
            pltpu.VMEM((32, UNITS, 16, WIDTH), BF16),
            pltpu.VMEM((32, 16, 128), F32),
            pltpu.VMEM((16, UNITS, 16, WIDTH), BF16),
            pltpu.VMEM((16, 16, 128), F32),
        ]
        + [pltpu.VMEM((SHARE, slots, units, 16, WIDTH), BF16) for slots, units in LANDING]
        + [pltpu.VMEM((slots, 4 * units, 128), F32) for slots, units in LANDING]
        + [pltpu.VMEM(*v) for v in HELD.values()]
        + [DMA(g), DMA(g), DMA((8,)), DMA((4,)), DMA((4,)), DMA((4,)), DMA((4,)), DMA(s), DMA(s)],
        compiler_params=pltpu.CompilerParams(collective_id=1, has_side_effects=True, vmem_limit_bytes=VMEM_LIMIT),
        name="layers",
    )(*args)


def finish_kernel(out, gz, total, small, out2, gz2, g_in, g_out, g_up, g_down, g_gains, g_vecs, g_mgain, g_mbias, g_heads):
    out2[...] = out[...]
    gz2[...] = gz[...]
    g_in[...] = total[IN : IN + 6]
    g_out[...] = total[OUT : OUT + 2]
    for q in range(4):
        g_down[:, :, q * 1024 : (q + 1) * 1024] = total[DOWN + 2 * q : DOWN + 2 * q + 2]
    g_up[...] = total[UP : UP + 8].reshape(128, WIDTH).T
    lane = lax.axis_index("dp") % 4
    thin = jnp.zeros((10, 32), F32)
    for j in range(4):
        thin = jnp.where(lane == j, small[0:10, 32 * j : 32 * (j + 1)], thin)
    for i in range(3):
        g_gains[i] = thin[i : i + 1]
    for i in range(7):
        g_vecs[i] = thin[3 + i : 4 + i]
    g_mgain[...] = small[10:11, :]
    g_mbias[...] = small[11:13, :]
    g_heads[...] = small[13:14, :16]


def finish(*args):
    f = jax.ShapeDtypeStruct
    return pl.pallas_call(
        finish_kernel,
        out_shape=[
            f((TOK, WIDTH), BF16), f((TOK, WIDTH), BF16), f((6, 16, WIDTH), F32), f((2, 16, WIDTH), F32),
            f((WIDTH, 128), F32), f((2, 16, FF), F32), f((3, 1, 32), F32), f((7, 1, 32), F32), f((1, 128), F32),
            f((2, 128), F32), f((1, 16), F32),
        ],
        in_specs=[VSPEC] * 4,
        out_specs=[VSPEC] * 11,
        name="finish",
    )(*args)


def body(
    tokens, cotangent, live_counts, segments, attn_input, attn_output, feed_up, feed_down,
    norm_gains, vector_bias, mid_gain, mid_bias, head_scale,
):
    res = run_layers(
        tokens, cotangent, live_counts, segments[None, :], attn_input[0].T.reshape(6, 16, WIDTH),
        attn_output[0].T.reshape(2, 16, WIDTH), feed_up[0], feed_down[0].T.reshape(2, 16, FF), norm_gains[0],
        vector_bias[0], mid_gain, mid_bias[0], head_scale,
    )
    out, gz, g_in, g_out, g_up, g_down, g_gains, g_vecs, g_mgain, g_mbias, g_heads = finish(*res)
    return (
        out[None],
        gz[None],
        g_in.reshape(96, WIDTH).T[None],
        g_out.reshape(32, WIDTH).T[None],
        g_up[None],
        g_down.reshape(32, FF).T[None],
        g_gains.transpose(1, 0, 2),
        g_vecs.transpose(1, 0, 2),
        g_mgain,
        g_mbias[None],
        g_heads,
    )


def solution(mesh):
    return jax.shard_map(
        body,
        mesh=mesh,
        in_specs=(
            P("dp", None), P("dp", None), P("dp"), P("dp"),
            P("pipe", None, "dp"), P("pipe", None, "dp"), P("pipe", None, "dp"), P("pipe", None, "dp"),
            P("pipe", None, "dp"), P("pipe", None, "dp"), P("pipe", "dp"), P("pipe", None, "dp"), P("pipe", None),
        ),
        out_specs=(
            P("pipe", "dp", None), P("pipe", "dp", None),
            P("pipe", None, "dp"), P("pipe", None, "dp"), P("pipe", None, "dp"), P("pipe", None, "dp"),
            P("pipe", None, "dp"), P("pipe", None, "dp"), P("pipe", "dp"), P("pipe", None, "dp"), P("pipe", None),
        ),
        check_vma=False,
    )
```

time: 407 us -> 283 us (0.70)
  Pallas kernels: 380 us -> 282 us
  local copies, waits for them, and re-layouts: 20 us -> 0 us
  other arithmetic: 5.11 us -> 0 us
    pallas_call x3 -> x2, Pallas kernels: 380 us -> 282 us  [the longest x1 279 us: run_layers(): pl.pallas_call(kernel, out_shape=[jax.ShapeDtypeStruct((TOK, WIDTH), BF16...]
    unnamed x13 -> x0, local copies, waits for them, and re-layouts: 11.6 us -> none
    broadcast_in_dim x7 -> x0, local copies, waits for them, and re-layouts: 4.94 us -> none  [the longest x1 1.39 us: body(): fwd = run_forward(own, tokens, segments[:, None], segments[None, :], hs)]
where the time goes in v2:
time: 283 us
  Pallas kernels  282 us (100%)
    pallas_call x1, Pallas kernels, run_layers(): pl.pallas_call(kernel, out_shape=[jax.ShapeDtypeStruct((TOK, WIDTH), BF16...  279 us

profile of v2, /device:TPU:0, one launch (start us, length us, event | category | flops | bytes accessed | tf_op | source)
XLA Modules:
  0.0 283.1 jit_solution(9771992038057528233)
XLA Ops:
  0.6 279.2 %layers.1 = (bf16[128,1024]{1,0:T(8,128)(2,1)}, bf16[128,1024]{1,0:T(8,128)(2,1)}, f32[24,16,1024]{2,1,0:T(8,128)}, f32[16,128]{1,0:T(8,128)}) custom-call(bf16[128,1024]{1,0:T(8,128)(2,1)} %refs_0_.1, bf16[128,1024]{1,0:T(8,128)(2,1)} %refs_1_.1, s32[2]{0:T(128)} %refs_2_.1, s32[1,128]{1,0:T(1,128)} %bitcast.47, bf16[6,16,1024]{2,1,0:T(8,128)(2,1)} %bitcast.43, ...), custom_call_target="tpu_custom_call" | custom-call | tf_op jit(solution)/shard_map/layers/pallas_call | solution.py:833
  279.8 3.2 %finish.1 = (bf16[128,1024]{1,0:T(8,128)(2,1)}, bf16[128,1024]{1,0:T(8,128)(2,1)}, f32[6,16,1024]{2,1,0:T(8,128)}, f32[2,16,1024]{2,1,0:T(8,128)}, f32[1024,128]...) custom-call(bf16[128,1024]{1,0:T(8,128)(2,1)} %get-tuple-element.26., ...), custom_call_target="tpu_custom_call" | custom-call | tf_op jit(solution)/shard_map/finish/pallas_call | solution.py:881
